TPU v7x, 32 devices: a whole 2x2x4 slice. The times are simulated.
32 devices in a mesh: seq: 8 (over z, core), tp: 4 (over y, x).
Axes of the slice: x: 2, y: 2, z: 4, core: 2. Of those that a mesh axis runs over, the one named last changes fastest.
Arguments:
- tokens: bfloat16 [4, 2048, 2048], P(None, 'seq'), may hold values from -6 to 6
- positions: int32 [4, 2048], P(None, 'seq'), may hold values from 0 to 2047, as said below
- w_query: bfloat16 [2048, 2048], P(None, 'tp'), may hold values from -0.1875 to 0.1875
- w_key: bfloat16 [2048, 2048], P(None, 'tp'), may hold values from -0.1875 to 0.1875
- w_value: bfloat16 [2048, 2048], P(None, 'tp'), may hold values from -0.125 to 0.125
- w_out: bfloat16 [2048, 2048], P('tp'), may hold values from -0.5 to 0.5
- w_gate: bfloat16 [2048, 5504], P(None, 'tp'), may hold values from -0.125 to 0.125
- w_up: bfloat16 [2048, 5504], P(None, 'tp'), may hold values from -0.125 to 0.125
- w_down: bfloat16 [5504, 2048], P('tp'), may hold values from -0.15625 to 0.15625
- gain_attn: float32 [2048], replicated, may hold values from 0.5 to 1.5
- gain_ffn: float32 [2048], replicated, may hold values from 0.5 to 1.5
- cotangent: bfloat16 [4, 2048, 2048], P(None, 'seq'), may hold values from -6 to 6
Outputs:
- output: bfloat16 [4, 2048, 2048], P(None, 'seq')
- token_grad: bfloat16 [4, 2048, 2048], P(None, 'seq')
- grad_query: float32 [2048, 2048], P(None, 'tp')
- grad_key: float32 [2048, 2048], P(None, 'tp')
- grad_value: float32 [2048, 2048], P(None, 'tp')
- grad_out: float32 [2048, 2048], P('tp')
- grad_gate: float32 [2048, 5504], P(None, 'tp')
- grad_up: float32 [2048, 5504], P(None, 'tp')
- grad_down: float32 [5504, 2048], P('tp')
- grad_gain_attn: float32 [2048], replicated
- grad_gain_ffn: float32 [2048], replicated
Inputs may be any that keep to these rules, and one draw needn't show every extreme that they name: Each row of 2048 tokens is a pack of documents: positions are 0 at a document's first token and rise by one to its end; every row begins a document at its first token, and in every draw one row holds a document that begins among its first 256 tokens and runs to the row's end.
All inputs are finite; a program needn't handle non-finite values.
Results may differ from a plain program's by a relative error of at most 0.02.
Values may be sent and summed in bfloat16 or wider, within the bound.
No kernel may reach another device: no remote copies, remote signals or barrier semaphores. Data moves between devices by JAX's collectives and lax.ppermute only.
A program may use at most 320 MiB of HBM per device.

v0:
```python
import jax
import jax.numpy as jnp
from jax import lax
from jax.sharding import PartitionSpec as P

HEAD = 128
WINDOW = 1024


EPS = 1e-05
THETA = 10000.0
NEG = -1e30


def passed_along(x, axis, by):
    peers = lax.axis_size(axis)
    pairs = [(i, i + by) for i in range(peers) if 0 <= i + by < peers]
    return lax.ppermute(x, axis, pairs)


def rotary_tables(positions, head_size):
    half_size = head_size // 2
    freq_table = THETA ** (-jnp.arange(half_size, dtype=jnp.float32) / half_size)
    angles = positions.astype(jnp.float32)[:, :, None, None] * freq_table
    cosine = jnp.cos(angles)
    sine_part = jnp.sin(angles)
    return (
        jnp.concatenate([cosine, cosine], axis=-1),
        jnp.concatenate([-sine_part, sine_part], axis=-1),
    )


def swap_halves(vectors):
    half_size = vectors.shape[-1] // 2
    return jnp.concatenate([vectors[..., half_size:], vectors[..., :half_size]], axis=-1)


def rotate(vectors, tables):
    return vectors * tables[0] + swap_halves(vectors) * tables[1]


def rotate_back(upstream, tables):
    return upstream * tables[0] + swap_halves(upstream * tables[1])


def norm_forward(inputs, gain_vec):
    inverse = lax.rsqrt(jnp.mean(inputs * inputs, axis=-1, keepdims=True) + EPS)
    return (inputs * inverse * gain_vec, inverse)


def norm_backward(upstream, inputs, inverse, gain_vec):
    plain_norm = inputs * inverse
    scaled = upstream * gain_vec
    inner_mean = jnp.mean(scaled * plain_norm, axis=-1, keepdims=True)
    return (inverse * (scaled - plain_norm * inner_mean), jnp.sum(upstream * plain_norm, axis=0))


def across(left_side, right_side):
    return lax.dot_general(
        left_side, right_side, (((0,), (0,)), ((), ())), preferred_element_type=jnp.float32
    )


def against(left_side, right_side):
    return lax.dot_general(
        left_side, right_side, (((1,), (1,)), ((), ())), preferred_element_type=jnp.float32
    )


def scores_of(queries, near_keys, positions):
    query_len = queries.shape[1]
    key_len = near_keys.shape[1]
    offset = jnp.arange(query_len)[:, None] - jnp.arange(key_len)[None, :] + WINDOW
    visible = (offset >= 0) & (offset < WINDOW) & (offset <= positions[:, :, None])
    raw_scores = jnp.einsum(
        "rqhd,rkhd->rhqk", queries, near_keys, preferred_element_type=jnp.float32
    ) * queries.shape[-1] ** (-0.5)
    return jnp.where(visible[:, None], raw_scores, NEG)


def attend(queries, near_pair, positions):
    scores = scores_of(queries, near_pair[0], positions)
    highest = jnp.max(scores, axis=-1, keepdims=True)
    log_total = highest + jnp.log(jnp.sum(jnp.exp(scores - highest), axis=-1, keepdims=True))
    weights = jnp.exp(scores - log_total).astype(jnp.bfloat16)
    mixed_heads = jnp.einsum(
        "rhqk,rkhd->rqhd", weights, near_pair[1], preferred_element_type=jnp.float32
    )
    return (mixed_heads, log_total)


def attend_back(queries, near_pair, positions, log_total, mixed_grad):
    near_keys = near_pair[0]
    near_values = near_pair[1]
    scores = scores_of(queries, near_keys, positions)
    probabilities = jnp.exp(scores - log_total)
    weights = probabilities.astype(jnp.bfloat16)
    weight_grad = jnp.einsum(
        "rqhd,rkhd->rhqk", mixed_grad, near_values, preferred_element_type=jnp.float32
    )
    delta_sum = jnp.sum(probabilities * weight_grad, axis=-1, keepdims=True)
    score_grad = (probabilities * (weight_grad - delta_sum)).astype(jnp.bfloat16)
    factor = queries.shape[-1] ** (-0.5)
    query_grad = (
        jnp.einsum("rhqk,rkhd->rqhd", score_grad, near_keys, preferred_element_type=jnp.float32)
        * factor
    )
    key_grad = (
        jnp.einsum("rhqk,rqhd->rkhd", score_grad, queries, preferred_element_type=jnp.float32)
        * factor
    )
    value_grad = jnp.einsum(
        "rhqk,rqhd->rkhd", weights, mixed_grad, preferred_element_type=jnp.float32
    )
    return (query_grad, jnp.stack([key_grad, value_grad]))


def fetch_halo(local_pair, halo_reach, mover):
    gathered = [local_pair]
    for stride in range(1, halo_reach + 1):
        gathered.insert(0, mover(local_pair, stride))
    return jnp.concatenate(gathered, axis=2)


def forward_move(piece, stride):
    return passed_along(piece, "seq", stride)


def backward_move(piece, stride):
    return passed_along(piece, "seq", stride)


def return_halo(pair_grad, halo_reach, span_size):
    own_grads = pair_grad[:, :, halo_reach * span_size :]
    for stride in range(1, halo_reach + 1):
        start_at = (halo_reach - stride) * span_size
        parcel = pair_grad[:, :, start_at : start_at + span_size]
        own_grads = own_grads + passed_along(parcel.astype(jnp.bfloat16), "seq", -stride).astype(
            parcel.dtype
        )
    return own_grads


def per_device(
    tokens,
    positions,
    w_query,
    w_key,
    w_value,
    w_out,
    w_gate,
    w_up,
    w_down,
    gain_attn,
    gain_ffn,
    cotangent,
):
    row_count, span_size, model_width = tokens.shape
    tok_count = row_count * span_size
    halo_reach = WINDOW // span_size
    head_count = w_query.shape[1] // HEAD

    def combine(partial_sum):
        return lax.psum(partial_sum, "tp")

    tok_float = tokens.reshape(tok_count, model_width).astype(jnp.float32)
    tables = rotary_tables(positions, HEAD)
    normed_attn, inverse_attn = norm_forward(tok_float, gain_attn)
    normed_attn = normed_attn.astype(jnp.bfloat16)
    head_shape = (row_count, span_size, head_count, HEAD)
    flat_heads = (tok_count, head_count * HEAD)

    def project(weight):
        return jnp.dot(normed_attn, weight, preferred_element_type=jnp.float32).reshape(head_shape)

    queries = rotate(project(w_query), tables).astype(jnp.bfloat16)
    local_pair = jnp.stack([rotate(project(w_key), tables), project(w_value)]).astype(jnp.bfloat16)
    near_pair = fetch_halo(local_pair, halo_reach, forward_move)
    mixed_heads, log_total = attend(queries, near_pair, positions)
    mixed_heads = mixed_heads.reshape(flat_heads).astype(jnp.bfloat16)
    attn_part = jnp.dot(mixed_heads, w_out, preferred_element_type=jnp.float32)
    residual = tok_float + combine(attn_part)
    normed_ffn, inverse_ffn = norm_forward(residual, gain_ffn)
    normed_ffn = normed_ffn.astype(jnp.bfloat16)
    gate_in = jnp.dot(normed_ffn, w_gate, preferred_element_type=jnp.float32)
    upward = jnp.dot(normed_ffn, w_up, preferred_element_type=jnp.float32)
    sigmoid_gate = jax.nn.sigmoid(gate_in)
    swish_gate = gate_in * sigmoid_gate
    activated = (swish_gate * upward).astype(jnp.bfloat16)
    ffn_part = jnp.dot(activated, w_down, preferred_element_type=jnp.float32)
    output = (residual + combine(ffn_part)).astype(jnp.bfloat16)
    upstream_low = cotangent.reshape(tok_count, model_width)
    upstream = upstream_low.astype(jnp.float32)
    down_w_grad = across(activated, upstream_low)
    act_grad = against(upstream_low, w_down)
    gate_grad = (
        act_grad * upward * (sigmoid_gate * (1.0 + gate_in * (1.0 - sigmoid_gate)))
    ).astype(jnp.bfloat16)
    up_grad = (act_grad * swish_gate).astype(jnp.bfloat16)
    gate_w_grad = across(normed_ffn, gate_grad)
    up_w_grad = across(normed_ffn, up_grad)
    ffn_back = against(gate_grad, w_gate) + against(up_grad, w_up)
    back_norm, gain_ffn_grad = norm_backward(combine(ffn_back), residual, inverse_ffn, gain_ffn)
    resid_grad = upstream + back_norm
    resid_low = resid_grad.astype(jnp.bfloat16)
    out_w_grad = across(mixed_heads, resid_low)
    mixed_grad = against(resid_low, w_out).astype(jnp.bfloat16).reshape(head_shape)
    back_pair = fetch_halo(local_pair, halo_reach, backward_move)
    query_grad, pair_grad = attend_back(queries, back_pair, positions, log_total, mixed_grad)
    pair_grad = return_halo(pair_grad, halo_reach, span_size)
    query_lin_grad = rotate_back(query_grad, tables).astype(jnp.bfloat16).reshape(flat_heads)
    key_lin_grad = rotate_back(pair_grad[0], tables).astype(jnp.bfloat16).reshape(flat_heads)
    value_lin_grad = pair_grad[1].astype(jnp.bfloat16).reshape(flat_heads)
    query_w_grad = across(normed_attn, query_lin_grad)
    key_w_grad = across(normed_attn, key_lin_grad)
    value_w_grad = across(normed_attn, value_lin_grad)
    attn_back = (
        against(query_lin_grad, w_query)
        + against(key_lin_grad, w_key)
        + against(value_lin_grad, w_value)
    )
    back_norm, gain_attn_grad = norm_backward(
        combine(attn_back), tok_float, inverse_attn, gain_attn
    )
    token_grad = (resid_grad + back_norm).astype(jnp.bfloat16)
    (
        sum_query,
        sum_key,
        sum_value,
        sum_out,
        sum_gate,
        sum_up,
        sum_down,
        sum_gain_attn,
        sum_gain_ffn,
    ) = (
        lax.psum_scatter(
            query_w_grad.astype(jnp.bfloat16), "seq", scatter_dimension=0, tiled=True
        ).astype(jnp.float32),
        lax.psum_scatter(
            key_w_grad.astype(jnp.bfloat16), "seq", scatter_dimension=0, tiled=True
        ).astype(jnp.float32),
        lax.psum_scatter(
            value_w_grad.astype(jnp.bfloat16), "seq", scatter_dimension=0, tiled=True
        ).astype(jnp.float32),
        lax.psum_scatter(
            out_w_grad.astype(jnp.bfloat16), "seq", scatter_dimension=1, tiled=True
        ).astype(jnp.float32),
        lax.psum_scatter(
            gate_w_grad.astype(jnp.bfloat16), "seq", scatter_dimension=0, tiled=True
        ).astype(jnp.float32),
        lax.psum_scatter(
            up_w_grad.astype(jnp.bfloat16), "seq", scatter_dimension=0, tiled=True
        ).astype(jnp.float32),
        lax.psum_scatter(
            down_w_grad.astype(jnp.bfloat16), "seq", scatter_dimension=1, tiled=True
        ).astype(jnp.float32),
        lax.psum_scatter(
            gain_attn_grad.astype(jnp.bfloat16), "seq", scatter_dimension=0, tiled=True
        ).astype(jnp.float32),
        lax.psum_scatter(
            gain_ffn_grad.astype(jnp.bfloat16), "seq", scatter_dimension=0, tiled=True
        ).astype(jnp.float32),
    )
    (
        full_query,
        full_key,
        full_value,
        full_out,
        full_gate,
        full_up,
        full_down,
        full_gain_attn,
        full_gain_ffn,
    ) = (
        lax.all_gather(sum_query.astype(jnp.bfloat16), "seq", axis=0, tiled=True).astype(
            sum_query.dtype
        ),
        lax.all_gather(sum_key.astype(jnp.bfloat16), "seq", axis=0, tiled=True).astype(
            sum_key.dtype
        ),
        lax.all_gather(sum_value.astype(jnp.bfloat16), "seq", axis=0, tiled=True).astype(
            sum_value.dtype
        ),
        lax.all_gather(sum_out.astype(jnp.bfloat16), "seq", axis=1, tiled=True).astype(
            sum_out.dtype
        ),
        lax.all_gather(sum_gate.astype(jnp.bfloat16), "seq", axis=0, tiled=True).astype(
            sum_gate.dtype
        ),
        lax.all_gather(sum_up.astype(jnp.bfloat16), "seq", axis=0, tiled=True).astype(sum_up.dtype),
        lax.all_gather(sum_down.astype(jnp.bfloat16), "seq", axis=1, tiled=True).astype(
            sum_down.dtype
        ),
        lax.all_gather(sum_gain_attn.astype(jnp.bfloat16), "seq", axis=0, tiled=True).astype(
            sum_gain_attn.dtype
        ),
        lax.all_gather(sum_gain_ffn.astype(jnp.bfloat16), "seq", axis=0, tiled=True).astype(
            sum_gain_ffn.dtype
        ),
    )
    return (
        output.reshape(row_count, span_size, model_width),
        token_grad.reshape(row_count, span_size, model_width),
        full_query,
        full_key,
        full_value,
        full_out,
        full_gate,
        full_up,
        full_down,
        full_gain_attn,
        full_gain_ffn,
    )


def solution(mesh):
    return jax.shard_map(
        per_device,
        mesh=mesh,
        in_specs=(
            P(None, "seq", None),
            P(None, "seq"),
            P(None, "tp"),
            P(None, "tp"),
            P(None, "tp"),
            P("tp", None),
            P(None, "tp"),
            P(None, "tp"),
            P("tp", None),
            P(),
            P(),
            P(None, "seq", None),
        ),
        out_specs=(
            P(None, "seq", None),
            P(None, "seq", None),
            P(None, "tp"),
            P(None, "tp"),
            P(None, "tp"),
            P("tp", None),
            P(None, "tp"),
            P(None, "tp"),
            P("tp", None),
            P(),
            P(),
        ),
        check_vma=False,
    )
```

profile of v0, /device:TPU:0, one launch (start us, length us, event | category | flops | bytes accessed | tf_op | source)
XLA Modules:
  0.0 2038.8 jit_solution(3681221483796109764)
XLA Ops:
  56.5 37.5 %collective-permute-done = bf16[2,4,256,4,128]{2,4,3,1,0:T(8,128)(2,1)S(1)} collective-permute-done((bf16[2,4,256,4,128]{2,4,3,1,0:T(8,128)(2,1)S(1)}, bf16[2,4,256,4,128]{2,4,3,1,0:T(8,128)(2,1)S(1)}, u32[]{:S(2)}, u32[]{:S(2)}) %collective-permute-start) | collective-permute-done | bytes 2097184 | tf_op jit(solution)/shard_map/ppermute | solution.py:18
  94.2 44.7 %collective-permute-done.1 = bf16[2,4,256,4,128]{2,4,3,1,0:T(8,128)(2,1)S(1)} collective-permute-done((bf16[2,4,256,4,128]{2,4,3,1,0:T(8,128)(2,1)S(1)}, bf16[2,4,256,4,128]{2,4,3,1,0:T(8,128)(2,1)S(1)}, u32[]{:S(2)}, u32[]{:S(2)}) %collective-permute-start.1) | collective-permute-done | bytes 2097184 | tf_op jit(solution)/shard_map/ppermute | solution.py:18
  139.1 44.7 %collective-permute-done.2 = bf16[2,4,256,4,128]{2,4,3,1,0:T(8,128)(2,1)S(1)} collective-permute-done((bf16[2,4,256,4,128]{2,4,3,1,0:T(8,128)(2,1)S(1)}, bf16[2,4,256,4,128]{2,4,3,1,0:T(8,128)(2,1)S(1)}, u32[]{:S(2)}, u32[]{:S(2)}) %collective-permute-start.2) | collective-permute-done | bytes 2097184 | tf_op jit(solution)/shard_map/ppermute | solution.py:18
  194.8 10.3 exponential_reduce_fusion
  205.1 10.3 fusion.51
  224.2 261.4 %all-reduce.8.cloned.1.call-done = f32[1024,2048]{1,0:T(8,128)} async-done(((f32[1024,2048]{1,0:T(8,128)}), f32[1024,2048]{1,0:T(8,128)}) %all-reduce.8.cloned.1.call-update) | async-done | bytes 8388624 | tf_op jit(solution)/shard_map/psum | solution.py:164
  496.9 11.0 fusion.84
  515.9 14.9 multiply_convert_fusion.2
  552.7 170.2 %all-reduce.10.cloned.1.call-done = f32[1024,2048]{1,0:T(8,128)} async-done(((f32[1024,2048]{1,0:T(8,128)}), f32[1024,2048]{1,0:T(8,128)}) %all-reduce.10.cloned.1.call-update) | async-done | bytes 8388624 | tf_op jit(solution)/shard_map/psum | solution.py:164
  743.5 14.9 multiply_reduce_fusion
  758.4 18.3 multiply_convert_fusion
  776.7 10.3 bitcast_multiply_fusion.4
  806.5 12.0 convolution_bitcast_fusion
  839.5 129.5 %collective-permute-done.7 = bf16[2,4,256,4,128]{2,4,3,1,0:T(8,128)(2,1)} collective-permute-done((bf16[2,4,256,4,128]{2,4,3,1,0:T(8,128)(2,1)}, bf16[2,4,256,4,128]{2,4,3,1,0:T(8,128)(2,1)}, u32[]{:S(2)}, u32[]{:S(2)}) %collective-permute-start.7) | collective-permute-done | bytes 2097184 | tf_op jit(solution)/shard_map/ppermute | solution.py:18
  994.4 10.2 convolution_convert_fusion.1
  1004.7 10.4 convolution_convert_fusion
  1015.2 10.2 convolution_convert_fusion.2
  1026.8 103.4 %reduce-scatter.10.cloned.1.call-done = bf16[256,512]{1,0:T(8,128)(2,1)} async-done(((bf16[2048,512]{1,0:T(8,128)(2,1)}), bf16[256,512]{1,0:T(8,128)(2,1)}) %reduce-scatter.10.cloned.1.call-update) | async-done | bytes 262160 | tf_op jit(solution)/shard_map/reduce_scatter | solution.py:240
  1130.3 36.6 %reduce-scatter.12.cloned.1.call-done = bf16[256,512]{1,0:T(8,128)(2,1)} async-done(((bf16[2048,512]{1,0:T(8,128)(2,1)}), bf16[256,512]{1,0:T(8,128)(2,1)}) %reduce-scatter.12.cloned.1.call-update) | async-done | bytes 262160 | tf_op jit(solution)/shard_map/reduce_scatter | solution.py:243
  1166.9 65.1 %reduce-scatter.16.cloned.1.call-done = bf16[256,1376]{0,1:T(8,128)(2,1)} async-done(((bf16[2048,1376]{0,1:T(8,128)(2,1)}), bf16[256,1376]{0,1:T(8,128)(2,1)}) %reduce-scatter.16.cloned.1.call-update) | async-done | bytes 704528 | tf_op jit(solution)/shard_map/reduce_scatter | solution.py:249
  1232.1 64.9 %reduce-scatter.18.cloned.1.call-done = bf16[256,1376]{0,1:T(8,128)(2,1)} async-done(((bf16[2048,1376]{0,1:T(8,128)(2,1)}), bf16[256,1376]{0,1:T(8,128)(2,1)}) %reduce-scatter.18.cloned.1.call-update) | async-done | bytes 704528 | tf_op jit(solution)/shard_map/reduce_scatter | solution.py:252
  1297.1 64.9 %reduce-scatter.20.cloned.1.call-done = bf16[1376,256]{1,0:T(8,128)(2,1)} async-done(((bf16[1376,2048]{1,0:T(8,128)(2,1)}), bf16[1376,256]{1,0:T(8,128)(2,1)}) %reduce-scatter.20.cloned.1.call-update) | async-done | bytes 704528 | tf_op jit(solution)/shard_map/reduce_scatter | solution.py:255
  1362.3 11.8 fusion.86
  1403.5 19.5 all-gather.16.cloned.1.call-done
  1427.2 25.6 %all-gather.12.cloned.1.call-done = bf16[2048,512]{1,0:T(8,128)(2,1)} async-done(((bf16[256,512]{1,0:T(8,128)(2,1)}), bf16[2048,512]{1,0:T(8,128)(2,1)}) %all-gather.12.cloned.1.call-update) | async-done | bytes 2097168 | tf_op jit(solution)/shard_map/all_gather | solution.py:279
  1457.0 26.1 %all-gather.14.cloned.1.call-done = bf16[2048,512]{1,0:T(8,128)(2,1)} async-done(((bf16[256,512]{1,0:T(8,128)(2,1)}), bf16[2048,512]{1,0:T(8,128)(2,1)}) %all-gather.14.cloned.1.call-update) | async-done | bytes 2097168 | tf_op jit(solution)/shard_map/all_gather | solution.py:282
  1487.3 56.6 %all-gather.18.cloned.1.call-done = bf16[2048,1376]{0,1:T(8,128)(2,1)} async-done(((bf16[256,1376]{0,1:T(8,128)(2,1)}), bf16[2048,1376]{0,1:T(8,128)(2,1)}) %all-gather.18.cloned.1.call-update) | async-done | bytes 5636112 | tf_op jit(solution)/shard_map/all_gather | solution.py:288
  1552.6 50.8 %all-gather.20.cloned.1.call-done = bf16[2048,1376]{0,1:T(8,128)(2,1)} async-done(((bf16[256,1376]{0,1:T(8,128)(2,1)}), bf16[2048,1376]{0,1:T(8,128)(2,1)}) %all-gather.20.cloned.1.call-update) | async-done | bytes 5636112 | tf_op jit(solution)/shard_map/all_gather | solution.py:291
  1612.1 50.8 %all-gather.22.cloned.1.call-done = bf16[1376,2048]{1,0:T(8,128)(2,1)} async-done(((bf16[1376,256]{1,0:T(8,128)(2,1)}), bf16[1376,2048]{1,0:T(8,128)(2,1)}) %all-gather.22.cloned.1.call-update) | async-done | bytes 5636112 | tf_op jit(solution)/shard_map/all_gather | solution.py:292
  1672.0 301.6 %all-reduce.12.cloned.1.call-done = (f32[1024,2048]{1,0:T(8,128)}, f32[1024,2048]{1,0:T(8,128)}) async-done(((f32[1024,2048]{1,0:T(8,128)}, f32[1024,2048]{1,0:T(8,128)}), (f32[1024,2048]{1,0:T(8,128)}, f32[1024,2048]{1,0:T(8,128)})) %all-reduce.12.cloned.1.call-update) | async-done | bytes 16777232 | tf_op jit(solution)/shard_map/psum | solution.py:164
  1995.0 16.6 all-reduce.3
  2020.8 10.4 all-gather.1
  (247 shorter events, 297.3 us)
Async XLA Ops:
  7.2 209.6 %copy-start = (bf16[512,2048]{1,0:T(8,128)(2,1)S(1)}, bf16[512,2048]{1,0:T(8,128)(2,1)}, u32[]{:S(2)}) copy-start(bf16[512,2048]{1,0:T(8,128)(2,1)} %param.17) | copy-start | bytes 6291460
  7.2 478.4 %all-reduce.8.cloned.1.call-start = ((), (), s32[]{:S(2)}) async-start(), calls=%async_computation.7 | async-start | bytes 16777216 | tf_op jit(solution)/shard_map/psum | solution.py:164
  41.8 142.7 %copy-start.11 = (bf16[4,256,4,128]{1,3,2,0:T(8,128)(2,1)}, bf16[4,256,4,128]{1,3,2,0:T(8,128)(2,1)S(1)}, u32[]{:S(2)}) copy-start(bf16[4,256,4,128]{1,3,2,0:T(8,128)(2,1)S(1)} %get-tuple-element.39) | copy-start | bytes 3145732
  42.0 52.0 %collective-permute-start = (bf16[2,4,256,4,128]{2,4,3,1,0:T(8,128)(2,1)S(1)}, bf16[2,4,256,4,128]{2,4,3,1,0:T(8,128)(2,1)S(1)}, u32[]{:S(2)}, u32[]{:S(2)}) collective-permute-start(bf16[2,4,256,4,128]{2,4,3,1,0:T(8,128)(2,1)S(1)} %pad_maximum_fusion.1), channel_id=1, source_target_pairs={{0,16},{4,20},{8,24},{12,28},{1,17},{5,21},{9,25},{13,29},{2,18},{... | collective-permute-start | bytes 6291464 | tf_op jit(solution)/shard_map/ppermute | solution.py:18
  48.3 90.7 %collective-permute-start.1 = (bf16[2,4,256,4,128]{2,4,3,1,0:T(8,128)(2,1)S(1)}, bf16[2,4,256,4,128]{2,4,3,1,0:T(8,128)(2,1)S(1)}, u32[]{:S(2)}, u32[]{:S(2)}) collective-permute-start(bf16[2,4,256,4,128]{2,4,3,1,0:T(8,128)(2,1)S(1)} %pad_maximum_fusion.1), channel_id=1, source_target_pairs={{0,12},{4,16},{8,20},{12,24},{16,28},{1,13},{5,17},{9,21},{13,25},... | collective-permute-start | bytes 6291464 | tf_op jit(solution)/shard_map/ppermute | solution.py:18
  51.1 132.8 %collective-permute-start.2 = (bf16[2,4,256,4,128]{2,4,3,1,0:T(8,128)(2,1)S(1)}, bf16[2,4,256,4,128]{2,4,3,1,0:T(8,128)(2,1)S(1)}, u32[]{:S(2)}, u32[]{:S(2)}) collective-permute-start(bf16[2,4,256,4,128]{2,4,3,1,0:T(8,128)(2,1)S(1)} %pad_maximum_fusion.1), channel_id=1, source_target_pairs={{0,8},{4,12},{8,16},{12,20},{16,24},{20,28},{1,9},{5,13},{9,17},{1... | collective-permute-start | bytes 6291464 | tf_op jit(solution)/shard_map/ppermute | solution.py:18
  53.3 130.7 %collective-permute-start.3 = (bf16[2,4,256,4,128]{2,4,3,1,0:T(8,128)(2,1)S(1)}, bf16[2,4,256,4,128]{2,4,3,1,0:T(8,128)(2,1)S(1)}, u32[]{:S(2)}, u32[]{:S(2)}) collective-permute-start(bf16[2,4,256,4,128]{2,4,3,1,0:T(8,128)(2,1)S(1)} %pad_maximum_fusion.1), channel_id=1, source_target_pairs={{0,4},{4,8},{8,12},{12,16},{16,20},{20,24},{24,28},{1,5},{5,9},{9,... | collective-permute-start | bytes 6291464 | tf_op jit(solution)/shard_map/ppermute | solution.py:18
  223.8 267.6 %copy-start.38 = (f32[2048]{0:T(1024)S(1)}, f32[2048]{0:T(1024)}, u32[]{:S(2)}) copy-start(f32[2048]{0:T(1024)} %param.22) | copy-start | bytes 24580
  223.8 499.2 %all-reduce.10.cloned.1.call-start = ((), (), s32[]{:S(2)}) async-start(), calls=%async_computation.8 | async-start | bytes 16777216 | tf_op jit(solution)/shard_map/psum | solution.py:164
  507.9 22.9 %slice-start.7 = ((s8[5636096]{0:T(1024)(128)(4,1)}), s8[4194304]{0:T(1024)(128)(4,1)S(1)}, s32[]{:S(2)}) async-start(s8[5636096]{0:T(1024)(128)(4,1)} %bitcast.232), calls=%async_computation.31 | async-start | bytes 8388608
  550.0 475.5 %reduce-scatter.8.cloned.1.call-start = ((), (), s32[]{:S(2)}) async-start(), calls=%async_computation.9 | async-start | bytes 2359296 | tf_op jit(solution)/shard_map/reduce_scatter | solution.py:237
  796.6 229.4 %reduce-scatter.14.cloned.1.call-start = ((), (), s32[]{:S(2)}) async-start(), calls=%async_computation.15 | async-start | bytes 2359296 | tf_op jit(solution)/shard_map/reduce_scatter | solution.py:246
  806.5 29.1 %slice-start = ((s8[8388608]{0:T(1024)(128)(4,1)}), s8[4194304]{0:T(1024)(128)(4,1)S(1)}, s32[]{:S(2)}) async-start(s8[8388608]{0:T(1024)(128)(4,1)} %bitcast.193), calls=%async_computation.24 | async-start | bytes 8388608
  830.4 138.6 %collective-permute-start.7 = (bf16[2,4,256,4,128]{2,4,3,1,0:T(8,128)(2,1)}, bf16[2,4,256,4,128]{2,4,3,1,0:T(8,128)(2,1)}, u32[]{:S(2)}, u32[]{:S(2)}) collective-permute-start(bf16[2,4,256,4,128]{2,4,3,1,0:T(8,128)(2,1)} %get-tuple-element.25), channel_id=1, source_target_pairs={{16,0},{20,4},{24,8},{28,12},{17,1},{21,5},{25,9},{29,13},{18,2},{... | collective-permute-start | bytes 6291464 | tf_op jit(solution)/shard_map/ppermute | solution.py:18
  831.7 137.3 %collective-permute-start.6 = (bf16[2,4,256,4,128]{2,4,3,1,0:T(8,128)(2,1)}, bf16[2,4,256,4,128]{2,4,3,1,0:T(8,128)(2,1)}, u32[]{:S(2)}, u32[]{:S(2)}) collective-permute-start(bf16[2,4,256,4,128]{2,4,3,1,0:T(8,128)(2,1)} %get-tuple-element.26), channel_id=1, source_target_pairs={{12,0},{16,4},{20,8},{24,12},{28,16},{13,1},{17,5},{21,9},{25,13},... | collective-permute-start | bytes 6291464 | tf_op jit(solution)/shard_map/ppermute | solution.py:18
  833.0 136.0 %collective-permute-start.5 = (bf16[2,4,256,4,128]{2,4,3,1,0:T(8,128)(2,1)}, bf16[2,4,256,4,128]{2,4,3,1,0:T(8,128)(2,1)}, u32[]{:S(2)}, u32[]{:S(2)}) collective-permute-start(bf16[2,4,256,4,128]{2,4,3,1,0:T(8,128)(2,1)} %get-tuple-element.27), channel_id=1, source_target_pairs={{8,0},{12,4},{16,8},{20,12},{24,16},{28,20},{9,1},{13,5},{17,9},{2... | collective-permute-start | bytes 6291464 | tf_op jit(solution)/shard_map/ppermute | solution.py:18
  834.3 134.7 %collective-permute-start.4 = (bf16[2,4,256,4,128]{2,4,3,1,0:T(8,128)(2,1)}, bf16[2,4,256,4,128]{2,4,3,1,0:T(8,128)(2,1)}, u32[]{:S(2)}, u32[]{:S(2)}) collective-permute-start(bf16[2,4,256,4,128]{2,4,3,1,0:T(8,128)(2,1)} %get-tuple-element.24), channel_id=1, source_target_pairs={{4,0},{8,4},{12,8},{16,12},{20,16},{24,20},{28,24},{5,1},{9,5},{13... | collective-permute-start | bytes 6291464 | tf_op jit(solution)/shard_map/ppermute | solution.py:18
  839.5 135.4 %copy-start.19 = (f32[4,256,128]{1,2,0:T(8,128)S(1)}, f32[4,256,128]{1,2,0:T(8,128)}, u32[]{:S(2)}) copy-start(f32[4,256,128]{1,2,0:T(8,128)} %copy-done.18) | copy-start | bytes 1572868
  839.5 290.7 %reduce-scatter.10.cloned.1.call-start = ((), (), s32[]{:S(2)}) async-start(), calls=%async_computation.11 | async-start | bytes 2359296 | tf_op jit(solution)/shard_map/reduce_scatter | solution.py:240
  985.5 181.4 %reduce-scatter.12.cloned.1.call-start = ((), (), s32[]{:S(2)}) async-start(), calls=%async_computation.13 | async-start | bytes 2359296 | tf_op jit(solution)/shard_map/reduce_scatter | solution.py:243
  994.4 237.7 %reduce-scatter.16.cloned.1.call-start = ((), (), s32[]{:S(2)}) async-start(), calls=%async_computation.17 | async-start | bytes 6340608 | tf_op jit(solution)/shard_map/reduce_scatter | solution.py:249
  1004.7 292.4 %reduce-scatter.18.cloned.1.call-start = ((), (), s32[]{:S(2)}) async-start(), calls=%async_computation.19 | async-start | bytes 6340608 | tf_op jit(solution)/shard_map/reduce_scatter | solution.py:252
  1015.2 346.8 %reduce-scatter.20.cloned.1.call-start = ((), (), s32[]{:S(2)}) async-start(), calls=%async_computation.21 | async-start | bytes 6340608 | tf_op jit(solution)/shard_map/reduce_scatter | solution.py:255
  1025.4 373.8 %all-gather.10.cloned.1.call-start = ((), (), s32[]{:S(2)}) async-start(), calls=%async_computation.10 | async-start | bytes 2359296 | tf_op jit(solution)/shard_map/all_gather | solution.py:276
  1026.0 397.0 %all-gather.16.cloned.1.call-start = ((), (), s32[]{:S(2)}) async-start(), calls=%async_computation.16 | async-start | bytes 2359296 | tf_op jit(solution)/shard_map/all_gather | solution.py:285
  1026.8 426.1 %all-gather.12.cloned.1.call-start = ((), (), s32[]{:S(2)}) async-start(), calls=%async_computation.12 | async-start | bytes 2359296 | tf_op jit(solution)/shard_map/all_gather | solution.py:279
  1130.2 352.9 %all-gather.14.cloned.1.call-start = ((), (), s32[]{:S(2)}) async-start(), calls=%async_computation.14 | async-start | bytes 2359296 | tf_op jit(solution)/shard_map/all_gather | solution.py:282
  1166.9 377.0 %all-gather.18.cloned.1.call-start = ((), (), s32[]{:S(2)}) async-start(), calls=%async_computation.18 | async-start | bytes 6340608 | tf_op jit(solution)/shard_map/all_gather | solution.py:288
  1232.1 371.3 %all-gather.20.cloned.1.call-start = ((), (), s32[]{:S(2)}) async-start(), calls=%async_computation.20 | async-start | bytes 6340608 | tf_op jit(solution)/shard_map/all_gather | solution.py:291
  1297.1 365.9 %all-gather.22.cloned.1.call-start = ((), (), s32[]{:S(2)}) async-start(), calls=%async_computation.22 | async-start | bytes 6340608 | tf_op jit(solution)/shard_map/all_gather | solution.py:292
  1362.0 611.5 %all-reduce.12.cloned.1.call-start = ((), (), s32[]{:S(2)}) async-start(), calls=%async_computation.23 | async-start | bytes 33554432 | tf_op jit(solution)/shard_map/psum | solution.py:164
  1988.8 43.0 %copy-start.1 = (bf16[512,2048]{1,0:T(8,128)(2,1)S(1)}, bf16[512,2048]{1,0:T(8,128)(2,1)}, u32[]{:S(2)}) copy-start(bf16[512,2048]{1,0:T(8,128)(2,1)} %param.17) | copy-start | bytes 6291460
  (47 other events, 281.7 us)
Sparse Core Ops, SparseCore 0:
  223.9 261.6 all-reduce.7
  550.1 172.7 all-reduce.9
  796.8 36.4 reduce-scatter.7
  839.6 82.9 reduce-scatter.13
  985.6 144.5 reduce-scatter.9
  1132.3 34.4 reduce-scatter.11
  1169.8 62.2 reduce-scatter.15
  1235.1 61.9 reduce-scatter.17
  1300.0 61.9 reduce-scatter.19
  1363.5 27.4 all-gather.9
  1392.7 30.3 all-gather.15
  1424.6 28.1 all-gather.11
  1454.5 28.5 all-gather.13
  1484.7 59.2 all-gather.17
  1545.5 57.9 all-gather.19
  1605.0 57.9 all-gather.21
  1667.1 306.4 all-reduce.11
where the time goes:
time: 2050 us; the launch traced here: 2040 us
  waiting for transfers between devices  1560 us (76%)
  matrix products  224 us (11%)
  other arithmetic  145 us (7%)
  local copies, waits for them, and re-layouts  44.1 us (2%)
  blocking collectives  35.4 us (2%)
    psum x3, waiting for transfers between devices, combine(): return lax.psum(partial_sum, 'tp')  733 us
    ppermute x8, waiting for transfers between devices, passed_along(): return lax.ppermute(x, axis, pairs)  256 us
    reduce_scatter x1, waiting for transfers between devices, per_device(): lax.psum_scatter(key_w_grad.astype(jnp.bfloat16), 'seq', scatter_dimensio...  103 us
    reduce_scatter x1, waiting for transfers between devices, per_device(): lax.psum_scatter(gate_w_grad.astype(jnp.bfloat16), 'seq', scatter_dimensi...  65.1 us
    reduce_scatter x1, waiting for transfers between devices, per_device(): lax.psum_scatter(up_w_grad.astype(jnp.bfloat16), 'seq', scatter_dimension...  64.9 us
    reduce_scatter x1, waiting for transfers between devices, per_device(): lax.psum_scatter(down_w_grad.astype(jnp.bfloat16), 'seq', scatter_dimensi...  64.9 us
    all_gather x1, waiting for transfers between devices, per_device(): lax.all_gather(sum_gate.astype(jnp.bfloat16), 'seq', axis=0, tiled=True)  56.6 us
    dot_general x7, matrix products, across(): lax.dot_general(left_side, right_side, (((0,), (0,)), ((), ())), preferre...  53.3 us
  transfers between devices with their start and end apart: 25, of which 18 were waited for; matrix products, arithmetic and copies ran while one was open for 8% of the time, Pallas kernels for 0%

commit v1 on v0

v1 whole, which is shorter than its diff:
```python
import functools
import math

import jax
import jax.numpy as jnp
from jax import lax
from jax.experimental import pallas as pl
from jax.experimental.pallas import tpu as pltpu
from jax.sharding import PartitionSpec as P

HEAD = 128
WINDOW = 1024
EPS = 1e-05
THETA = 10000.0
NEG = -1e30
LOG2E = 1.4426950408889634
BF16 = jnp.bfloat16
F32 = jnp.float32


def tp_send(x, mask):
    peers = lax.axis_size("tp")
    return lax.ppermute(x, "tp", [(i, i ^ mask) for i in range(peers)])


def seq_shift(x, by):
    peers = lax.axis_size("seq")
    return lax.ppermute(x, "seq", [(i, i + by) for i in range(peers) if 0 <= i + by < peers])


def core_swap(x):
    peers = lax.axis_size("seq")
    return lax.ppermute(x, "seq", [(i, i ^ 1) for i in range(peers)])


def chip_step(x, by, active):
    pairs = [(2 * c + k, 2 * (c + by) + k) for c in active for k in range(2)]
    return lax.ppermute(x, "seq", pairs)


def halo(x, reach, sign):
    spans = [x]
    core = lax.axis_index("seq") % 2
    if lax.axis_size("seq") % 2 or reach % 2:
        return spans + [seq_shift(x, sign * d) for d in range(1, reach + 1)]
    sender = 0 if sign > 0 else 1
    for _ in range(reach // 2):
        near = spans[-1]
        far = seq_shift(near, 2 * sign)
        between = core_swap(jnp.where(core == sender, near, far))
        spans += [between, far]
    return spans


def small_halo(x, reach, sign):
    return [x] + [seq_shift(x, sign * d) for d in range(1, reach + 1)]


def tp_gather(x):
    peers = lax.axis_size("tp")
    if peers != 4:
        return [x] + [tp_send(x, m) for m in range(1, peers)]
    half = x.shape[0] // 2
    a, b = x[:half], x[half:]
    a_x = tp_send(a, 1)
    b_y = tp_send(b, 2)
    a_y = tp_send(a, 2)
    b_x = tp_send(b, 1)
    a_xy = tp_send(a_x, 2)
    b_xy = tp_send(b_y, 1)
    join = lambda u, v: jnp.concatenate([u, v], axis=0)
    return [x, join(a_x, b_x), join(a_y, b_y), join(a_xy, b_xy)]


def tp_reduce(part):
    pieces = part
    peers = lax.axis_size("tp")
    rows = pieces.shape[0] // peers
    piece = lambda m: pieces[m * rows : (m + 1) * rows]
    if peers != 4:
        total = piece(0).astype(F32)
        for m in range(1, peers):
            total = total + tp_send(piece(m), m).astype(F32)
        return total
    half = rows // 2
    top = lambda m: pieces[m * rows : m * rows + half]
    low = lambda m: pieces[m * rows + half : (m + 1) * rows]
    a3 = tp_send(top(3), 1)
    b3 = tp_send(low(3), 2)
    a1 = tp_send(top(1), 1)
    b2 = tp_send(low(2), 2)
    a2 = tp_send((top(2).astype(F32) + a3.astype(F32)).astype(BF16), 2)
    b1 = tp_send((low(1).astype(F32) + b3.astype(F32)).astype(BF16), 1)
    upper = top(0).astype(F32) + a1.astype(F32) + a2.astype(F32)
    lower = low(0).astype(F32) + b2.astype(F32) + b1.astype(F32)
    return jnp.concatenate([upper, lower], axis=0)


def place(pieces):
    peers = len(pieces)
    t = lax.axis_index("tp")
    rows, width = pieces[0].shape
    out = jnp.zeros((peers * rows, width), pieces[0].dtype)
    for m, piece in enumerate(pieces):
        out = lax.dynamic_update_slice(out, piece, ((t ^ m) * rows, 0))
    return out


def seq_total(half_of, axis):
    chips = lax.axis_size("seq") // 2
    s = lax.axis_index("seq")
    k, c = s % 2, s // 2
    from_core = core_swap(half_of(1 - k).astype(BF16))
    acc = (half_of(k) + from_core.astype(F32)).astype(BF16)
    width = acc.shape[axis] // chips
    shard = lambda i: lax.dynamic_slice_in_dim(acc, i * width, width, axis)
    right = left = None
    for step in range(1, chips):
        send_r = shard(jnp.clip(chips - step + c, 0, chips - 1))
        send_l = shard(jnp.clip(c + step - chips, 0, chips - 1))
        if step > 1:
            send_r = (send_r.astype(F32) + right.astype(F32)).astype(BF16)
            send_l = (send_l.astype(F32) + left.astype(F32)).astype(BF16)
        right = chip_step(send_r, 1, range(0, step))
        left = chip_step(send_l, -1, range(chips - step, chips))
    own = (shard(c).astype(F32) + right.astype(F32) + left.astype(F32)).astype(BF16)
    before, after = [], []
    cur_r = cur_l = own
    for step in range(1, chips):
        cur_r = chip_step(cur_r, 1, range(step - 1, chips - 1))
        cur_l = chip_step(cur_l, -1, range(1, chips - step + 1))
        before.insert(0, cur_r)
        after.append(cur_l)
    line = jnp.concatenate(before + [own] + after, axis=axis)
    mine = lax.dynamic_slice_in_dim(line, (chips - 1 - c) * width, chips * width, axis)
    theirs = core_swap(mine)
    first = jnp.where(k == 0, mine, theirs).astype(F32)
    second = jnp.where(k == 0, theirs, mine).astype(F32)
    return jnp.concatenate([first, second], axis=axis)


def dot_tt(a, b):
    return lax.dot_general(a, b, (((1,), (1,)), ((), ())), preferred_element_type=F32)


def dot_nn(a, b):
    return lax.dot_general(a, b, (((1,), (0,)), ((), ())), preferred_element_type=F32)


def swap_lanes(x):
    half = x.shape[-1] // 2
    return jnp.concatenate([x[:, half:], x[:, :half]], axis=-1)


def attend_kernel(reach, low_ref, q_ref, *refs):
    k_refs, v_refs = refs[: reach + 1], refs[reach + 1 : 2 * reach + 2]
    out_ref, lse_ref = refs[2 * reach + 2 :]
    span = q_ref.shape[0]
    c = HEAD ** (-0.5) * LOG2E
    q = q_ref[...]
    low = low_ref[...]
    key = lax.broadcasted_iota(jnp.int32, (span, span), 1)
    scores = []
    for d in range(reach + 1):
        s = dot_tt(q, k_refs[d][...])
        seen = key >= low + d * span
        if d == 0:
            seen = seen & (key <= lax.broadcasted_iota(jnp.int32, (span, span), 0))
        scores.append(jnp.where(seen, s, NEG))
    top = functools.reduce(jnp.maximum, scores)
    top = jnp.max(top, axis=-1, keepdims=True)
    total = jnp.zeros((span, span), F32)
    mixed = jnp.zeros((span, HEAD), F32)
    for d in range(reach + 1):
        e = jnp.exp2((scores[d] - top) * c)
        total = total + e
        mixed = mixed + dot_nn(e.astype(BF16), v_refs[d][...])
    total = jnp.sum(total, axis=-1, keepdims=True)
    out_ref[...] = (mixed / total).astype(BF16)
    lse = top * c + jnp.log2(total)
    lse_ref[...] = jnp.transpose(jnp.broadcast_to(lse, (span, 128)))[:1][None, None]


def attend(queries, spans, low_col, rows):
    tokens, flat = queries.shape
    reach = len(spans) - 1
    heads = flat // HEAD
    span = tokens // rows
    head_spec = pl.BlockSpec((span, HEAD), lambda r, h: (r, h))
    value_spec = pl.BlockSpec((span, HEAD), lambda r, h: (r, heads + h))
    pairs = rows * heads * span * span * (reach + 1)
    return pl.pallas_call(
        functools.partial(attend_kernel, reach),
        grid=(rows, heads),
        in_specs=[pl.BlockSpec((span, 1), lambda r, h: (r, 0)), head_spec]
        + [head_spec] * (reach + 1)
        + [value_spec] * (reach + 1),
        out_specs=[head_spec, pl.BlockSpec((1, 1, 1, span), lambda r, h: (r, h, 0, 0))],
        out_shape=[
            jax.ShapeDtypeStruct((tokens, flat), BF16),
            jax.ShapeDtypeStruct((rows, heads, 1, span), F32),
        ],
        compiler_params=pltpu.CompilerParams(vmem_limit_bytes=48 * 1024 * 1024),
        cost_estimate=pl.CostEstimate(
            flops=8 * pairs * HEAD, bytes_accessed=16 * 1024 * 1024, transcendentals=pairs
        ),
        name="attend",
    )(low_col, queries, *spans, *spans)


def query_back_kernel(reach, low_ref, cos_ref, sin_ref, lse_ref, q_ref, g_ref, o_ref, *refs):
    k_refs, v_refs = refs[: reach + 1], refs[reach + 1 : 2 * reach + 2]
    (out_ref,) = refs[2 * reach + 2 :]
    span = q_ref.shape[0]
    c = HEAD ** (-0.5) * LOG2E
    q = q_ref[...]
    g = g_ref[...]
    low = low_ref[...]
    lse = jnp.transpose(jnp.broadcast_to(lse_ref[0, 0], (128, span)))[:, :1]
    delta = jnp.sum(g.astype(F32) * o_ref[...].astype(F32), axis=-1, keepdims=True)
    key = lax.broadcasted_iota(jnp.int32, (span, span), 1)
    grad = jnp.zeros((span, HEAD), F32)
    for d in range(reach + 1):
        keys = k_refs[d][...]
        s = dot_tt(q, keys)
        seen = key >= low + d * span
        if d == 0:
            seen = seen & (key <= lax.broadcasted_iota(jnp.int32, (span, span), 0))
        p = jnp.where(seen, jnp.exp2(s * c - lse), 0.0)
        dp = dot_tt(g, v_refs[d][...])
        ds = (p * (dp - delta)).astype(BF16)
        grad = grad + dot_nn(ds, keys)
    grad = grad * HEAD ** (-0.5)
    out_ref[...] = (grad * cos_ref[...] + swap_lanes(grad * sin_ref[...])).astype(BF16)


def query_back(queries, mixed_grad, mixed, spans, lse, low_col, tables, rows):
    tokens, flat = queries.shape
    reach = len(spans) - 1
    heads = flat // HEAD
    span = tokens // rows
    head_spec = pl.BlockSpec((span, HEAD), lambda r, h: (r, h))
    value_spec = pl.BlockSpec((span, HEAD), lambda r, h: (r, heads + h))
    table_spec = pl.BlockSpec((span, HEAD), lambda r, h: (r, 0))
    pairs = rows * heads * span * span * (reach + 1)
    return pl.pallas_call(
        functools.partial(query_back_kernel, reach),
        grid=(rows, heads),
        in_specs=[
            pl.BlockSpec((span, 1), lambda r, h: (r, 0)),
            table_spec,
            table_spec,
            pl.BlockSpec((1, 1, 1, span), lambda r, h: (r, h, 0, 0)),
            head_spec,
            head_spec,
            head_spec,
        ]
        + [head_spec] * (reach + 1)
        + [value_spec] * (reach + 1),
        out_specs=head_spec,
        out_shape=jax.ShapeDtypeStruct((tokens, flat), BF16),
        compiler_params=pltpu.CompilerParams(vmem_limit_bytes=48 * 1024 * 1024),
        cost_estimate=pl.CostEstimate(
            flops=12 * pairs * HEAD, bytes_accessed=20 * 1024 * 1024, transcendentals=pairs
        ),
        name="query_back",
    )(low_col, *tables, lse, queries, mixed_grad, mixed, *spans, *spans)


def key_back_kernel(reach, cos_ref, sin_ref, k_ref, v_ref, *refs):
    n = reach + 1
    low_refs, lse_refs, delta_refs, q_refs, g_refs = [refs[i * n : (i + 1) * n] for i in range(5)]
    key_out, value_out = refs[5 * n :]
    span = k_ref.shape[0]
    c = HEAD ** (-0.5) * LOG2E
    keys = k_ref[...]
    values = v_ref[...]
    key = lax.broadcasted_iota(jnp.int32, (span, span), 0)
    key_grad = jnp.zeros((span, HEAD), F32)
    value_grad = jnp.zeros((span, HEAD), F32)
    for d in range(n):
        q = q_refs[d][...]
        g = g_refs[d][...]
        s = dot_tt(keys, q)
        seen = key >= low_refs[d][0] + d * span
        if d == 0:
            seen = seen & (key <= lax.broadcasted_iota(jnp.int32, (span, span), 1))
        p = jnp.where(seen, jnp.exp2(s * c - lse_refs[d][0, 0]), 0.0)
        value_grad = value_grad + dot_nn(p.astype(BF16), g)
        dp = dot_tt(values, g)
        ds = (p * (dp - delta_refs[d][0, 0])).astype(BF16)
        key_grad = key_grad + dot_nn(ds, q)
    key_grad = key_grad * HEAD ** (-0.5)
    key_out[...] = (key_grad * cos_ref[...] + swap_lanes(key_grad * sin_ref[...])).astype(BF16)
    value_out[...] = value_grad.astype(BF16)


def key_back(pair, lows, lses, deltas, queries, grads, tables, rows):
    tokens, flat = queries[0].shape
    n = len(queries)
    heads = flat // HEAD
    span = tokens // rows
    head_spec = pl.BlockSpec((span, HEAD), lambda r, h: (r, h))
    value_spec = pl.BlockSpec((span, HEAD), lambda r, h: (r, heads + h))
    table_spec = pl.BlockSpec((span, HEAD), lambda r, h: (r, 0))
    low_spec = pl.BlockSpec((1, 1, span), lambda r, h: (r, 0, 0))
    stat_spec = pl.BlockSpec((1, 1, 1, span), lambda r, h: (r, h, 0, 0))
    pairs = rows * heads * span * span * n
    return pl.pallas_call(
        functools.partial(key_back_kernel, n - 1),
        grid=(rows, heads),
        in_specs=[table_spec, table_spec, head_spec, value_spec]
        + [low_spec] * n
        + [stat_spec] * (2 * n)
        + [head_spec] * (2 * n),
        out_specs=[head_spec, head_spec],
        out_shape=[jax.ShapeDtypeStruct((tokens, flat), BF16)] * 2,
        compiler_params=pltpu.CompilerParams(vmem_limit_bytes=48 * 1024 * 1024),
        cost_estimate=pl.CostEstimate(
            flops=16 * pairs * HEAD, bytes_accessed=20 * 1024 * 1024, transcendentals=pairs
        ),
        name="key_back",
    )(*tables, pair, pair, *lows, *lses, *deltas, *queries, *grads)


def across(left_side, right_side):
    return lax.dot_general(
        left_side, right_side, (((0,), (0,)), ((), ())), preferred_element_type=F32
    )


def against(left_side, right_side):
    return dot_tt(left_side, right_side)


def inverse_rms(v):
    return lax.rsqrt(jnp.mean(v * v, axis=-1, keepdims=True) + EPS)


def norm_backward(upstream, inputs, inverse, gain_vec):
    plain_norm = inputs * inverse
    scaled = upstream * gain_vec
    inner_mean = jnp.mean(scaled * plain_norm, axis=-1, keepdims=True)
    return (inverse * (scaled - plain_norm * inner_mean), jnp.sum(upstream * plain_norm, axis=0))


def half_columns(x, k):
    width = x.shape[1] // 2
    return lax.dynamic_slice_in_dim(x, k * width, width, 1)


def per_device(
    tokens,
    positions,
    w_query,
    w_key,
    w_value,
    w_out,
    w_gate,
    w_up,
    w_down,
    gain_attn,
    gain_ffn,
    cotangent,
):
    rows, span, width = tokens.shape
    count = rows * span
    peers = lax.axis_size("tp")
    own = count // peers
    t = lax.axis_index("tp")
    reach = WINDOW // span
    flat = w_query.shape[1]
    heads = flat // HEAD

    def reorder(x):
        parts = x.reshape((peers, rows // peers) + x.shape[1:])
        picked = [lax.dynamic_index_in_dim(parts, t ^ m, 0, keepdims=False) for m in range(peers)]
        return jnp.concatenate(picked, axis=0)

    out_rows = [w_out] + [tp_send(w_out, m) for m in range(1, peers)]

    place_of = reorder(positions)
    within = jnp.arange(span, dtype=jnp.int32)[None, :]
    low = jnp.maximum(within - place_of, within - (WINDOW - 1))
    low_col = low.reshape(count, 1)
    lows = small_halo(low.reshape(rows, 1, span), reach, -1)

    half_size = HEAD // 2
    freq = THETA ** (-jnp.arange(half_size, dtype=F32) / half_size)
    angles = place_of.reshape(count, 1).astype(F32) * freq
    cosine, sine = jnp.cos(angles), jnp.sin(angles)
    tables = (
        jnp.concatenate([cosine, cosine], axis=-1),
        jnp.concatenate([-sine, sine], axis=-1),
    )

    def rotate(lin):
        vectors = lin.reshape(count, heads, HEAD)
        swapped = jnp.concatenate([vectors[..., half_size:], vectors[..., :half_size]], axis=-1)
        return (vectors * tables[0][:, None] + swapped * tables[1][:, None]).reshape(count, flat)

    tok = reorder(tokens).reshape(count, width).astype(F32)
    normed_attn = (tok * inverse_rms(tok) * gain_attn).astype(BF16)
    tok_own = tok[:own]

    pair = jnp.concatenate(
        [rotate(dot_nn(normed_attn, w_key)), dot_nn(normed_attn, w_value)], axis=1
    ).astype(BF16)
    spans = halo(pair, reach, 1)
    queries = rotate(dot_nn(normed_attn, w_query)).astype(BF16)
    later_queries = halo(queries, reach, -1)

    upstream_low = reorder(cotangent).reshape(count, width)
    act_grad = against(upstream_low, w_down)

    mixed, lse = attend(queries, spans, low_col, rows)
    lses = small_halo(lse, reach, -1)

    mixed_own = [mixed[:own]]
    mixed_own += [tp_send(mixed[m * own : (m + 1) * own], m) for m in range(1, peers)]
    residual = tok_own
    for m in range(peers):
        residual = residual + dot_nn(mixed_own[m], out_rows[m])
    inverse_ffn = inverse_rms(residual)
    normed_own = (residual * inverse_ffn * gain_ffn).astype(BF16)
    normed_ffn = jnp.concatenate(tp_gather(normed_own), axis=0)

    gate_in = dot_nn(normed_ffn, w_gate)
    upward = dot_nn(normed_ffn, w_up)
    sigmoid_gate = jax.nn.sigmoid(gate_in)
    swish_gate = gate_in * sigmoid_gate
    activated = (swish_gate * upward).astype(BF16)
    gate_grad = (
        act_grad * upward * (sigmoid_gate * (1.0 + gate_in * (1.0 - sigmoid_gate)))
    ).astype(BF16)
    up_grad = (act_grad * swish_gate).astype(BF16)

    full_down = seq_total(lambda k: across(activated, half_columns(upstream_low, k)), 1)

    ffn_back = (against(gate_grad, w_gate) + against(up_grad, w_up)).astype(BF16)
    ffn_back = tp_reduce(ffn_back)
    back_norm, gain_ffn_grad = norm_backward(ffn_back, residual, inverse_ffn, gain_ffn)
    upstream_own = upstream_low[:own].astype(F32)
    resid_grad = upstream_own + back_norm
    resid_low = resid_grad.astype(BF16)

    grads_own = [against(resid_low, out_rows[m]).astype(BF16) for m in range(peers)]
    mixed_grad = jnp.concatenate(
        [grads_own[0]] + [tp_send(grads_own[m], m) for m in range(1, peers)], axis=0
    )
    later_grads = halo(mixed_grad, reach, -1)
    delta = jnp.sum(
        (mixed_grad.astype(F32) * mixed.astype(F32)).reshape(rows, span, heads, HEAD), axis=-1
    )
    delta = jnp.transpose(delta, (0, 2, 1)).reshape(rows, heads, 1, span)
    deltas = small_halo(delta, reach, -1)

    full_gate = seq_total(lambda k: across(half_columns(normed_ffn, k), gate_grad), 0)
    full_up = seq_total(lambda k: across(half_columns(normed_ffn, k), up_grad), 0)

    ffn_part = dot_nn(activated, w_down).astype(BF16)
    output = (residual + tp_reduce(ffn_part)).astype(BF16)
    output = place(tp_gather(output))

    resid_all = jnp.concatenate(tp_gather(resid_low), axis=0)

    query_grad = query_back(queries, mixed_grad, mixed, spans, lse, low_col, tables, rows)
    key_grad, value_grad = key_back(
        pair, lows, lses, deltas, later_queries, later_grads, tables, rows
    )

    full_out = seq_total(lambda k: across(half_columns(mixed, k), resid_all), 0)
    full_query = seq_total(lambda k: across(half_columns(normed_attn, k), query_grad), 0)
    full_key = seq_total(lambda k: across(half_columns(normed_attn, k), key_grad), 0)
    full_value = seq_total(lambda k: across(half_columns(normed_attn, k), value_grad), 0)

    attn_back = (
        against(query_grad, w_query) + against(key_grad, w_key) + against(value_grad, w_value)
    ).astype(BF16)
    attn_back = tp_reduce(attn_back)
    back_norm, gain_attn_grad = norm_backward(
        attn_back, tok_own, inverse_rms(tok_own), gain_attn
    )
    token_grad = place(tp_gather((resid_grad + back_norm).astype(BF16)))

    gain_grads = lax.psum(jnp.stack([gain_attn_grad, gain_ffn_grad]), ("seq", "tp"))
    return (
        output.reshape(rows, span, width),
        token_grad.reshape(rows, span, width),
        full_query,
        full_key,
        full_value,
        full_out,
        full_gate,
        full_up,
        full_down,
        gain_grads[0],
        gain_grads[1],
    )


def solution(mesh):
    return jax.shard_map(
        per_device,
        mesh=mesh,
        in_specs=(
            P(None, "seq", None),
            P(None, "seq"),
            P(None, "tp"),
            P(None, "tp"),
            P(None, "tp"),
            P("tp", None),
            P(None, "tp"),
            P(None, "tp"),
            P("tp", None),
            P(),
            P(),
            P(None, "seq", None),
        ),
        out_specs=(
            P(None, "seq", None),
            P(None, "seq", None),
            P(None, "tp"),
            P(None, "tp"),
            P(None, "tp"),
            P("tp", None),
            P(None, "tp"),
            P(None, "tp"),
            P("tp", None),
            P(),
            P(),
        ),
        check_vma=False,
    )
```

time: 2050 us -> 1230 us (0.60)
  waiting for transfers between devices: 1560 us -> 473 us
  starting transfers between devices: 19.4 us -> 313 us
  matrix products: 224 us -> 151 us
  Pallas kernels: 0 us -> 63.1 us
  other arithmetic: 145 us -> 107 us
  local copies, waits for them, and re-layouts: 44.1 us -> 65.5 us
    psum x3 -> x0, waiting for transfers between devices: 733 us -> none  [combine(): return lax.psum(partial_sum, 'tp')]
    reduce_scatter x7 -> x0, waiting for transfers between devices: 335 us -> none  [the longest x1 103 us: per_device(): lax.psum_scatter(key_w_grad.astype(jnp.bfloat16), 'seq', scatter_dimensio...]
    ppermute x8 -> x173, starting transfers between devices: 18.3 us -> 313 us  [the longest x84 206 us: chip_step(): return lax.ppermute(x, 'seq', pairs)]
    all_gather x7 -> x0, waiting for transfers between devices: 229 us -> none  [the longest x1 56.6 us: per_device(): lax.all_gather(sum_gate.astype(jnp.bfloat16), 'seq', axis=0, tiled=True)]
    ppermute x8 -> x173, waiting for transfers between devices: 256 us -> 473 us  [the longest x84 197 us: chip_step(): return lax.ppermute(x, 'seq', pairs)]
    pallas_call x0 -> x3, Pallas kernels: none -> 63.1 us  [the longest x1 22.8 us: key_back(): pl.pallas_call(functools.partial(key_back_kernel, n - 1), grid=(rows, hea...]
    dot_general x20, matrix products: 170 us -> 109 us  [the longest x10 59.6 us: dot_tt(): lax.dot_general(a, b, (((1,), (1,)), ((), ())), preferred_element_type=F32)]
    convert_element_type x17 -> x34, other arithmetic: 86.9 us -> 31.1 us  [the longest x14 9.66 us: seq_total(): send_r = (send_r.astype(F32) + right.astype(F32)).astype(BF16)]
  transfers between devices with their start and end apart: 25 -> 173, of which waited for: 18 -> 60; matrix products, arithmetic and copies ran while one was open for 8% -> 17% of each run, Pallas kernels for 0% -> 5%
where the time goes in v1:
time: 1230 us; the launch traced here: 1220 us
  waiting for transfers between devices  473 us (38%)
  starting transfers between devices  313 us (25%)
  matrix products  151 us (12%)
  other arithmetic  107 us (9%)
  local copies, waits for them, and re-layouts  65.5 us (5%)
  Pallas kernels  63.1 us (5%)
  blocking collectives  40.5 us (3%)
    ppermute x84, starting transfers between devices, chip_step(): return lax.ppermute(x, 'seq', pairs)  206 us
    ppermute x84, waiting for transfers between devices, chip_step(): return lax.ppermute(x, 'seq', pairs)  197 us
    ppermute x51, waiting for transfers between devices, tp_send(): return lax.ppermute(x, 'tp', [(i, i ^ mask) for i in range(peers)])  152 us
    ppermute x18, waiting for transfers between devices, seq_shift(): lax.ppermute(x, 'seq', [(i, i + by) for i in range(peers) if 0 <= i + by...  124 us
    ppermute x51, starting transfers between devices, tp_send(): return lax.ppermute(x, 'tp', [(i, i ^ mask) for i in range(peers)])  63.5 us
    dot_general x10, matrix products, dot_tt(): lax.dot_general(a, b, (((1,), (1,)), ((), ())), preferred_element_type=F32)  59.6 us
    dot_general x10, matrix products, dot_nn(): lax.dot_general(a, b, (((1,), (0,)), ((), ())), preferred_element_type=F32)  49.5 us
    dot_general x14, matrix products, across(): lax.dot_general(left_side, right_side, (((0,), (0,)), ((), ())), preferre...  42.3 us
  transfers between devices with their start and end apart: 173, of which 60 were waited for; matrix products, arithmetic and copies ran while one was open for 17% of the time, Pallas kernels for 5%

profile of v1, /device:TPU:0, one launch (start us, length us, event | category | flops | bytes accessed | tf_op | source)
XLA Modules:
  0.0 1217.8 jit_solution(15271998903273006648)
XLA Ops:
  53.6 42.2 %collective-permute-done.refs_2_.refs_7_ = bf16[1024,1024]{1,0:T(8,128)(2,1)} collective-permute-done((bf16[1024,1024]{1,0:T(8,128)(2,1)S(1)}, bf16[1024,1024]{1,0:T(8,128)(2,1)}, u32[]{:S(2)}, u32[]{:S(2)}) %collective-permute-start) | collective-permute-done | bytes 2097184 | tf_op jit(solution)/shard_map/ppermute | solution.py:28
  112.0 32.6 %collective-permute-done.2.refs_4_.refs_9_ = bf16[1024,1024]{1,0:T(8,128)(2,1)} collective-permute-done((bf16[1024,1024]{1,0:T(8,128)(2,1)}, bf16[1024,1024]{1,0:T(8,128)(2,1)}, u32[]{:S(2)}, u32[]{:S(2)}) %collective-permute-start.2) | collective-permute-done | bytes 2097184 | tf_op jit(solution)/shard_map/ppermute | solution.py:28
  164.5 17.8 %attend.1 = (bf16[1024,512]{1,0:T(8,128)(2,1)S(1)}, f32[4,4,1,256]{3,2,1,0:T(1,128)S(1)}) custom-call(s32[1024,1]{1,0:T(8,128)S(1)} %bitcast.110, bf16[1024,512]{1,0:T(8,128)(2,1)S(1)} %copy.51.q_ref.refs_15_, bf16[1024,1024]{1,0:T(8,128)(2,1)S(1)} %copy-done.2, bf16[1024,1024]{1,0:T(8,128)(2,1)} %collective-permute-done.1.refs_1_.refs_6_, ...), custom_call_target="tpu_custom_call" | custom-call | flops 5368709120 | bytes 16777216 | tf_op jit(solution)/shard_map/attend/pallas_call | solution.py:192
  191.7 12.9 %collective-permute-done.8 = bf16[256,512]{1,0:T(8,128)(2,1)S(1)} collective-permute-done((bf16[256,512]{1,0:T(8,128)(2,1)}, bf16[256,512]{1,0:T(8,128)(2,1)S(1)}, u32[]{:S(2)}, u32[]{:S(2)}) %collective-permute-start.8) | collective-permute-done | bytes 262176 | tf_op jit(solution)/shard_map/ppermute | solution.py:23
  235.6 9.2 collective-permute-done.11
  245.5 9.7 collective-permute-done.14
  263.2 12.8 %multiply_convert_fusion.1 = (bf16[1024,1376]{0,1:T(8,128)(2,1)S(1)}, bf16[1024,1376]{0,1:T(8,128)(2,1)}, bf16[1024,1376]{0,1:T(8,128)(2,1)}) fusion(f32[1024,1376]{0,1:T(8,128)} %fusion.87, f32[1024,1376]{0,1:T(8,128)} %fusion.86, bf16[1024,2048]{1,0:T(8,128)(2,1)S(1)} %constant_dynamic-update-slice_fusion, bf16[2048,1376]{0,1:T(8,128)(2,1)S(1)} %bitcast.140), kind=kOutput, calls=%fused_computation.13 | convolution fusion | flops 5792497664 | bytes 29556736 | tf_op jit(solution)/shard_map/dot_general | solution.py:147
  276.0 11.3 fusion.88
  287.3 11.2 add_convert_fusion.1
  301.2 9.0 convolution_convert_fusion
  345.3 13.5 %collective-permute-done.20 = bf16[128,2048]{1,0:T(8,128)(2,1)S(1)} collective-permute-done((bf16[128,2048]{1,0:T(8,128)(2,1)S(1)}, bf16[128,2048]{1,0:T(8,128)(2,1)S(1)}, u32[]{:S(2)}, u32[]{:S(2)}) %collective-permute-start.20) | collective-permute-done | bytes 524320 | tf_op jit(solution)/shard_map/ppermute | solution.py:23
  360.5 17.8 %collective-permute-done.18 = bf16[128,2048]{1,0:T(8,128)(2,1)S(1)} collective-permute-done((bf16[128,2048]{1,0:T(8,128)(2,1)S(1)}, bf16[128,2048]{1,0:T(8,128)(2,1)S(1)}, u32[]{:S(2)}, u32[]{:S(2)}) %collective-permute-start.18) | collective-permute-done | bytes 524320 | tf_op jit(solution)/shard_map/ppermute | solution.py:23
  381.1 8.5 collective-permute-done.21
  422.2 22.5 %query_back.1 = bf16[1024,512]{1,0:T(8,128)(2,1)S(1)} custom-call(s32[1024,1]{1,0:T(8,128)S(1)} %bitcast.111, f32[1024,128]{1,0:T(8,128)S(1)} %copy-done.7, f32[1024,128]{1,0:T(8,128)S(1)} %copy-done.10, f32[4,4,1,256]{3,2,1,0:T(1,128)S(1)} %get-tuple-element.16.lse_ref.refs_5_, bf16[1024,512]{1,0:T(8,128)(2,1)S(1)} %copy.51.q_ref.refs_15_, ...), custom_call_target="tpu_custom_call" | custom-call | flops 8053063680 | bytes 20971520 | tf_op jit(solution)/shard_map/query_back/pallas_call | solution.py:246
  478.6 11.2 collective-permute-done.114
  572.1 11.5 collective-permute-done.146
  623.7 9.8 collective-permute-done.133
  650.7 16.6 %collective-permute-done.76 = bf16[256,512]{1,0:T(8,128)(2,1)S(1)} collective-permute-done((bf16[256,512]{1,0:T(8,128)(2,1)S(1)}, bf16[256,512]{1,0:T(8,128)(2,1)S(1)}, u32[]{:S(2)}, u32[]{:S(2)}) %collective-permute-start.76) | collective-permute-done | bytes 262176 | tf_op jit(solution)/shard_map/ppermute | solution.py:38
  700.6 11.9 collective-permute-done.39.refs_3_
  733.7 23.7 %collective-permute-done.44.refs_9_ = f32[4,4,1,256]{3,2,1,0:T(1,128)S(1)} collective-permute-done((f32[4,4,1,256]{3,2,1,0:T(1,128)S(1)}, f32[4,4,1,256]{3,2,1,0:T(1,128)S(1)}, u32[]{:S(2)}, u32[]{:S(2)}) %collective-permute-start.44) | collective-permute-done | bytes 16416 | tf_op jit(solution)/shard_map/ppermute | solution.py:28
  777.4 22.8 %key_back.1 = (bf16[1024,512]{1,0:T(8,128)(2,1)S(1)}, bf16[1024,512]{1,0:T(8,128)(2,1)S(1)}) custom-call(f32[1024,128]{1,0:T(8,128)S(1)} %copy-done.8, f32[1024,128]{1,0:T(8,128)S(1)} %copy-done.11, bf16[1024,1024]{1,0:T(8,128)(2,1)} %copy-done.1, bf16[1024,1024]{1,0:T(8,128)(2,1)} %copy-done.1, s32[4,1,256]{2,1,0:T(1,128)S(1)} %fusion.67.refs_0_, ...), custom_call_target="tpu_custom_call" | custom-call | flops 10737418240 | bytes 20971520 | tf_op jit(solution)/shard_map/key_back/pallas_call | solution.py:309
  840.1 17.0 %collective-permute-done.129 = bf16[64,2048]{1,0:T(8,128)(2,1)S(1)} collective-permute-done((bf16[64,2048]{1,0:T(8,128)(2,1)S(1)}, bf16[64,2048]{1,0:T(8,128)(2,1)S(1)}, u32[]{:S(2)}, u32[]{:S(2)}) %collective-permute-start.129) | collective-permute-done | bytes 262176 | tf_op jit(solution)/shard_map/ppermute | solution.py:38
  864.8 12.8 %collective-permute-done.151 = bf16[256,1376]{0,1:T(8,128)(2,1)S(1)} collective-permute-done((bf16[256,1376]{0,1:T(8,128)(2,1)S(1)}, bf16[256,1376]{0,1:T(8,128)(2,1)S(1)}, u32[]{:S(2)}, u32[]{:S(2)}) %collective-permute-start.151) | collective-permute-done | bytes 704544 | tf_op jit(solution)/shard_map/ppermute | solution.py:38
  891.3 10.8 collective-permute-done.59
  936.0 40.5 %psum.7 = f32[2,2048]{1,0:T(2,128)S(1)} all-reduce(f32[2,2048]{1,0:T(2,128)S(1)} %pad_maximum_fusion.7), channel_id=1, replica_groups=mesh['seq'=8,'tp'=4] {'seq','tp'}, use_global_device_ids=true, to_apply=%region_8.9 | all-reduce | flops 4096 | bytes 32768 | tf_op jit(solution)/shard_map/psum | solution.py:486
  989.1 11.5 collective-permute-done.99
  1020.1 11.4 collective-permute-start.100
  1058.4 13.5 %collective-permute-done.142 = bf16[256,1376]{0,1:T(8,128)(2,1)S(1)} collective-permute-done((bf16[256,1376]{0,1:T(8,128)(2,1)}, bf16[256,1376]{0,1:T(8,128)(2,1)S(1)}, u32[]{:S(2)}, u32[]{:S(2)}) %collective-permute-start.142) | collective-permute-done | bytes 704544 | tf_op jit(solution)/shard_map/ppermute | solution.py:38
  1074.5 12.5 %collective-permute-done.156 = bf16[256,1376]{0,1:T(8,128)(2,1)S(1)} collective-permute-done((bf16[256,1376]{0,1:T(8,128)(2,1)S(1)}, bf16[256,1376]{0,1:T(8,128)(2,1)S(1)}, u32[]{:S(2)}, u32[]{:S(2)}) %collective-permute-start.156) | collective-permute-done | bytes 704544 | tf_op jit(solution)/shard_map/ppermute | solution.py:38
  1089.0 19.0 %collective-permute-start.168 = (bf16[1376,256]{1,0:T(8,128)(2,1)S(1)}, bf16[1376,256]{1,0:T(8,128)(2,1)S(1)}, u32[]{:S(2)}, u32[]{:S(2)}) collective-permute-start(bf16[1376,256]{1,0:T(8,128)(2,1)S(1)} %collective-permute-done.167), channel_id=1, source_target_pairs={{16,24},{20,28},{17,25},{21,29},{18,26},{22,30},{19,27},{23,31}} | collective-permute-start | bytes 2113544 | tf_op jit(solution)/shard_map/ppermute | solution.py:38
  1139.6 9.2 collective-permute-start.171
  1153.9 19.6 %collective-permute-done.95 = bf16[256,512]{1,0:T(8,128)(2,1)S(1)} collective-permute-done((bf16[256,512]{1,0:T(8,128)(2,1)S(1)}, bf16[256,512]{1,0:T(8,128)(2,1)S(1)}, u32[]{:S(2)}, u32[]{:S(2)}) %collective-permute-start.95) | collective-permute-done | bytes 262176 | tf_op jit(solution)/shard_map/ppermute | solution.py:38
  (759 shorter events, 696.8 us)
Async XLA Ops:
  46.0 49.8 %collective-permute-start = (bf16[1024,1024]{1,0:T(8,128)(2,1)S(1)}, bf16[1024,1024]{1,0:T(8,128)(2,1)}, u32[]{:S(2)}, u32[]{:S(2)}) collective-permute-start(bf16[1024,1024]{1,0:T(8,128)(2,1)S(1)} %pad_maximum_fusion.1.refs_0_.refs_5_.k_ref.v_ref), channel_id=1, source_target_pairs={{0,8},{4,12},{8,16},{12,20},{16,24},{20,28},{1,9},{5,13},{9,17},{1... | collective-permute-start | bytes 6291464 | tf_op jit(solution)/shard_map/ppermute | solution.py:28
  95.8 48.8 %collective-permute-start.2 = (bf16[1024,1024]{1,0:T(8,128)(2,1)}, bf16[1024,1024]{1,0:T(8,128)(2,1)}, u32[]{:S(2)}, u32[]{:S(2)}) collective-permute-start(bf16[1024,1024]{1,0:T(8,128)(2,1)} %collective-permute-done.refs_2_.refs_7_), channel_id=1, source_target_pairs={{0,8},{4,12},{8,16},{12,20},{16,24},{20,28},{1,9},{5,13},{9,17},{1... | collective-permute-start | bytes 6291464 | tf_op jit(solution)/shard_map/ppermute | solution.py:28
  101.6 88.7 %collective-permute-start.9 = (bf16[512,2048]{1,0:T(8,128)(2,1)}, bf16[512,2048]{1,0:T(8,128)(2,1)}, u32[]{:S(2)}, u32[]{:S(2)}) collective-permute-start(bf16[512,2048]{1,0:T(8,128)(2,1)} %param.17), channel_id=1, source_target_pairs={{0,3},{1,2},{2,1},{3,0},{4,7},{5,6},{6,5},{7,4},{8,11},{9,10},{10,... | collective-permute-start | bytes 6291464 | tf_op jit(solution)/shard_map/ppermute | solution.py:23
  104.9 102.5 %collective-permute-start.7 = (bf16[512,2048]{1,0:T(8,128)(2,1)}, bf16[512,2048]{1,0:T(8,128)(2,1)}, u32[]{:S(2)}, u32[]{:S(2)}) collective-permute-start(bf16[512,2048]{1,0:T(8,128)(2,1)} %param.17), channel_id=1, source_target_pairs={{0,2},{1,3},{2,0},{3,1},{4,6},{5,7},{6,4},{7,5},{8,10},{9,11},{10,... | collective-permute-start | bytes 6291464 | tf_op jit(solution)/shard_map/ppermute | solution.py:23
  106.8 104.8 %collective-permute-start.5 = (bf16[512,2048]{1,0:T(8,128)(2,1)}, bf16[512,2048]{1,0:T(8,128)(2,1)}, u32[]{:S(2)}, u32[]{:S(2)}) collective-permute-start(bf16[512,2048]{1,0:T(8,128)(2,1)} %param.17), channel_id=1, source_target_pairs={{0,1},{1,0},{2,3},{3,2},{4,5},{5,4},{6,7},{7,6},{8,9},{9,8},{10,11... | collective-permute-start | bytes 6291464 | tf_op jit(solution)/shard_map/ppermute | solution.py:23
  327.8 52.5 %collective-permute-start.31 = (bf16[128,2048]{1,0:T(8,128)(2,1)S(1)}, bf16[128,2048]{1,0:T(8,128)(2,1)S(1)}, u32[]{:S(2)}, u32[]{:S(2)}) collective-permute-start(bf16[128,2048]{1,0:T(8,128)(2,1)S(1)} %get-tuple-element.51), channel_id=1, source_target_pairs={{0,2},{1,3},{2,0},{3,1},{4,6},{5,7},{6,4},{7,5},{8,10},{9,11},{10,... | collective-permute-start | bytes 1572872 | tf_op jit(solution)/shard_map/ppermute | solution.py:23
  336.0 45.1 %collective-permute-start.19 = (bf16[128,2048]{1,0:T(8,128)(2,1)S(1)}, bf16[128,2048]{1,0:T(8,128)(2,1)S(1)}, u32[]{:S(2)}, u32[]{:S(2)}) collective-permute-start(bf16[128,2048]{1,0:T(8,128)(2,1)S(1)} %get-tuple-element.61), channel_id=1, source_target_pairs={{0,2},{1,3},{2,0},{3,1},{4,6},{5,7},{6,4},{7,5},{8,10},{9,11},{10,... | collective-permute-start | bytes 1572872 | tf_op jit(solution)/shard_map/ppermute | solution.py:23
  345.3 176.8 %collective-permute-start.131 = (bf16[1024,1376]{0,1:T(8,128)(2,1)}, bf16[1024,1376]{0,1:T(8,128)(2,1)}, u32[]{:S(2)}, u32[]{:S(2)}) collective-permute-start(bf16[1024,1376]{0,1:T(8,128)(2,1)} %convolution_convert_fusion.2), channel_id=1, source_target_pairs={{0,4},{4,0},{8,12},{12,8},{16,20},{20,16},{24,28},{28,24},{1,5},{5... | collective-permute-start | bytes 8454152 | tf_op jit(solution)/shard_map/ppermute | solution.py:33
  394.5 58.3 %collective-permute-start.23 = (bf16[128,2048]{1,0:T(8,128)(2,1)}, bf16[128,2048]{1,0:T(8,128)(2,1)}, u32[]{:S(2)}, u32[]{:S(2)}) collective-permute-start(bf16[128,2048]{1,0:T(8,128)(2,1)} %get-tuple-element.120), channel_id=1, source_target_pairs={{0,1},{1,0},{2,3},{3,2},{4,5},{5,4},{6,7},{7,6},{8,9},{9,8},{10,11... | collective-permute-start | bytes 1572872 | tf_op jit(solution)/shard_map/ppermute | solution.py:23
  415.9 48.9 %collective-permute-start.25 = (bf16[128,2048]{1,0:T(8,128)(2,1)}, bf16[128,2048]{1,0:T(8,128)(2,1)}, u32[]{:S(2)}, u32[]{:S(2)}) collective-permute-start(bf16[128,2048]{1,0:T(8,128)(2,1)} %get-tuple-element.120), channel_id=1, source_target_pairs={{0,2},{1,3},{2,0},{3,1},{4,6},{5,7},{6,4},{7,5},{8,10},{9,11},{10,... | collective-permute-start | bytes 1572872 | tf_op jit(solution)/shard_map/ppermute | solution.py:23
  416.7 46.8 %collective-permute-start.22 = (bf16[128,2048]{1,0:T(8,128)(2,1)}, bf16[128,2048]{1,0:T(8,128)(2,1)}, u32[]{:S(2)}, u32[]{:S(2)}) collective-permute-start(bf16[128,2048]{1,0:T(8,128)(2,1)} %get-tuple-element.119), channel_id=1, source_target_pairs={{0,1},{1,0},{2,3},{3,2},{4,5},{5,4},{6,7},{7,6},{8,9},{9,8},{10,11... | collective-permute-start | bytes 1572872 | tf_op jit(solution)/shard_map/ppermute | solution.py:23
  420.8 47.1 %collective-permute-start.111 = (bf16[128,2048]{1,0:T(8,128)(2,1)}, bf16[128,2048]{1,0:T(8,128)(2,1)}, u32[]{:S(2)}, u32[]{:S(2)}) collective-permute-start(bf16[128,2048]{1,0:T(8,128)(2,1)} %get-tuple-element.100), channel_id=1, source_target_pairs={{0,1},{1,0},{2,3},{3,2},{4,5},{5,4},{6,7},{7,6},{8,9},{9,8},{10,11... | collective-permute-start | bytes 1572872 | tf_op jit(solution)/shard_map/ppermute | solution.py:23
  478.6 48.9 %collective-permute-start.145 = (bf16[1024,1376]{0,1:T(8,128)(2,1)S(1)}, bf16[1024,1376]{0,1:T(8,128)(2,1)S(1)}, u32[]{:S(2)}, u32[]{:S(2)}) collective-permute-start(bf16[1024,1376]{0,1:T(8,128)(2,1)S(1)} %copy-done.89), channel_id=1, source_target_pairs={{0,4},{4,0},{8,12},{12,8},{16,20},{20,16},{24,28},{28,24},{1,5},{5... | collective-permute-start | bytes 8454152 | tf_op jit(solution)/shard_map/ppermute | solution.py:33
  510.1 182.1 %collective-permute-start.37 = (s32[4,1,256]{2,1,0:T(1,128)S(1)}, s32[4,1,256]{2,1,0:T(1,128)S(1)}, u32[]{:S(2)}, u32[]{:S(2)}) collective-permute-start(s32[4,1,256]{2,1,0:T(1,128)S(1)} %fusion.67.refs_0_), channel_id=1, source_target_pairs={{4,0},{8,4},{12,8},{16,12},{20,16},{24,20},{28,24},{5,1},{9,5},{13... | collective-permute-start | bytes 12296 | tf_op jit(solution)/shard_map/ppermute | solution.py:28
  516.1 51.4 %collective-permute-start.53 = (bf16[1024,512]{1,0:T(8,128)(2,1)S(1)}, bf16[1024,512]{1,0:T(8,128)(2,1)S(1)}, u32[]{:S(2)}, u32[]{:S(2)}) collective-permute-start(bf16[1024,512]{1,0:T(8,128)(2,1)S(1)} %copy-done.15), channel_id=1, source_target_pairs={{8,0},{12,4},{16,8},{20,12},{24,16},{28,20},{9,1},{13,5},{17,9},{2... | collective-permute-start | bytes 3145736 | tf_op jit(solution)/shard_map/ppermute | solution.py:28
  623.0 46.3 %collective-permute-start.163 = (bf16[1376,256]{1,0:T(8,128)(2,1)S(1)}, bf16[1376,256]{1,0:T(8,128)(2,1)S(1)}, u32[]{:S(2)}, u32[]{:S(2)}) collective-permute-start(bf16[1376,256]{1,0:T(8,128)(2,1)S(1)} %get-tuple-element.70), channel_id=1, source_target_pairs={{24,16},{28,20},{25,17},{29,21},{26,18},{30,22},{27,19},{31,23}} | collective-permute-start | bytes 2113544 | tf_op jit(solution)/shard_map/ppermute | solution.py:38
  633.5 45.6 %collective-permute-start.161 = (bf16[1376,256]{1,0:T(8,128)(2,1)S(1)}, bf16[1376,256]{1,0:T(8,128)(2,1)S(1)}, u32[]{:S(2)}, u32[]{:S(2)}) collective-permute-start(bf16[1376,256]{1,0:T(8,128)(2,1)S(1)} %add_convert_fusion.13), channel_id=1, source_target_pairs={{0,8},{4,12},{8,16},{12,20},{1,9},{5,13},{9,17},{13,21},{2,10},{6,... | collective-permute-start | bytes 2113544 | tf_op jit(solution)/shard_map/ppermute | solution.py:38
  724.3 51.5 %collective-permute-start.54 = (bf16[1024,512]{1,0:T(8,128)(2,1)S(1)}, bf16[1024,512]{1,0:T(8,128)(2,1)S(1)}, u32[]{:S(2)}, u32[]{:S(2)}) collective-permute-start(bf16[1024,512]{1,0:T(8,128)(2,1)S(1)} %get-tuple-element.116), channel_id=1, source_target_pairs={{0,4},{4,0},{8,12},{12,8},{16,20},{20,16},{24,28},{28,24},{1,5},{5... | collective-permute-start | bytes 3145736 | tf_op jit(solution)/shard_map/ppermute | solution.py:33
  727.3 50.1 %collective-permute-start.56 = (bf16[1024,512]{1,0:T(8,128)(2,1)S(1)}, bf16[1024,512]{1,0:T(8,128)(2,1)}, u32[]{:S(2)}, u32[]{:S(2)}) collective-permute-start(bf16[1024,512]{1,0:T(8,128)(2,1)S(1)} %get-tuple-element.115), channel_id=1, source_target_pairs={{0,4},{4,0},{8,12},{12,8},{16,20},{20,16},{24,28},{28,24},{1,5},{5... | collective-permute-start | bytes 3145736 | tf_op jit(solution)/shard_map/ppermute | solution.py:33
  763.0 96.6 %collective-permute-start.134 = (bf16[256,1376]{0,1:T(8,128)(2,1)}, bf16[256,1376]{0,1:T(8,128)(2,1)}, u32[]{:S(2)}, u32[]{:S(2)}) collective-permute-start(bf16[256,1376]{0,1:T(8,128)(2,1)} %get-tuple-element.75), channel_id=1, source_target_pairs={{0,8},{4,12},{8,16},{12,20},{16,24},{20,28},{1,9},{5,13},{9,17},{1... | collective-permute-start | bytes 2113544 | tf_op jit(solution)/shard_map/ppermute | solution.py:38
  767.8 95.6 %collective-permute-start.148 = (bf16[256,1376]{0,1:T(8,128)(2,1)}, bf16[256,1376]{0,1:T(8,128)(2,1)}, u32[]{:S(2)}, u32[]{:S(2)}) collective-permute-start(bf16[256,1376]{0,1:T(8,128)(2,1)} %get-tuple-element.71), channel_id=1, source_target_pairs={{0,8},{4,12},{8,16},{12,20},{16,24},{20,28},{1,9},{5,13},{9,17},{1... | collective-permute-start | bytes 2113544 | tf_op jit(solution)/shard_map/ppermute | solution.py:38
  772.2 45.6 %collective-permute-start.124 = (bf16[64,2048]{1,0:T(8,128)(2,1)S(1)}, bf16[64,2048]{1,0:T(8,128)(2,1)}, u32[]{:S(2)}, u32[]{:S(2)}) collective-permute-start(bf16[64,2048]{1,0:T(8,128)(2,1)S(1)} %add_convert_fusion.30), channel_id=1, source_target_pairs={{0,8},{4,12},{8,16},{12,20},{16,24},{20,28},{1,9},{5,13},{9,17},{1... | collective-permute-start | bytes 786440 | tf_op jit(solution)/shard_map/ppermute | solution.py:38
  775.8 44.1 %collective-permute-start.127 = (bf16[64,2048]{1,0:T(8,128)(2,1)S(1)}, bf16[64,2048]{1,0:T(8,128)(2,1)}, u32[]{:S(2)}, u32[]{:S(2)}) collective-permute-start(bf16[64,2048]{1,0:T(8,128)(2,1)S(1)} %add_convert_fusion.30), channel_id=1, source_target_pairs={{8,0},{12,4},{16,8},{20,12},{24,16},{28,20},{9,1},{13,5},{17,9},{2... | collective-permute-start | bytes 786440 | tf_op jit(solution)/shard_map/ppermute | solution.py:38
  820.0 61.5 %collective-permute-start.162 = (bf16[1376,256]{1,0:T(8,128)(2,1)S(1)}, bf16[1376,256]{1,0:T(8,128)(2,1)S(1)}, u32[]{:S(2)}, u32[]{:S(2)}) collective-permute-start(bf16[1376,256]{1,0:T(8,128)(2,1)S(1)} %copy-done.72), channel_id=1, source_target_pairs={{0,8},{4,12},{8,16},{12,20},{16,24},{20,28},{1,9},{5,13},{9,17},{1... | collective-permute-start | bytes 2113544 | tf_op jit(solution)/shard_map/ppermute | solution.py:38
  891.1 118.1 %collective-permute-start.130 = (bf16[256,2048]{1,0:T(8,128)(2,1)}, bf16[256,2048]{1,0:T(8,128)(2,1)}, u32[]{:S(2)}, u32[]{:S(2)}) collective-permute-start(bf16[256,2048]{1,0:T(8,128)(2,1)} %constant_dynamic-slice_fusion.9), channel_id=1, source_target_pairs={{0,4},{4,0},{8,12},{12,8},{16,20},{20,16},{24,28},{28,24},{1,5},{5... | collective-permute-start | bytes 3145736 | tf_op jit(solution)/shard_map/ppermute | solution.py:33
  914.0 64.4 %collective-permute-start.138 = (bf16[256,1376]{0,1:T(8,128)(2,1)}, bf16[256,1376]{0,1:T(8,128)(2,1)}, u32[]{:S(2)}, u32[]{:S(2)}) collective-permute-start(bf16[256,1376]{0,1:T(8,128)(2,1)} %add_convert_fusion.19), channel_id=1, source_target_pairs={{0,8},{4,12},{8,16},{12,20},{16,24},{20,28},{1,9},{5,13},{9,17},{1... | collective-permute-start | bytes 2113544 | tf_op jit(solution)/shard_map/ppermute | solution.py:38
  921.6 54.9 %collective-permute-start.101 = (bf16[256,512]{1,0:T(8,128)(2,1)S(1)}, bf16[256,512]{1,0:T(8,128)(2,1)}, u32[]{:S(2)}, u32[]{:S(2)}) collective-permute-start(bf16[256,512]{1,0:T(8,128)(2,1)S(1)} %get-tuple-element.104), channel_id=1, source_target_pairs={{24,16},{28,20},{25,17},{29,21},{26,18},{30,22},{27,19},{31,23}} | collective-permute-start | bytes 786440 | tf_op jit(solution)/shard_map/ppermute | solution.py:38
  922.9 56.8 %collective-permute-start.85 = (bf16[256,512]{1,0:T(8,128)(2,1)}, bf16[256,512]{1,0:T(8,128)(2,1)}, u32[]{:S(2)}, u32[]{:S(2)}) collective-permute-start(bf16[256,512]{1,0:T(8,128)(2,1)} %add_convert_fusion.44), channel_id=1, source_target_pairs={{0,8},{4,12},{8,16},{12,20},{1,9},{5,13},{9,17},{13,21},{2,10},{6,... | collective-permute-start | bytes 786440 | tf_op jit(solution)/shard_map/ppermute | solution.py:38
  934.7 51.6 %collective-permute-start.141 = (bf16[256,1376]{0,1:T(8,128)(2,1)}, bf16[256,1376]{0,1:T(8,128)(2,1)}, u32[]{:S(2)}, u32[]{:S(2)}) collective-permute-start(bf16[256,1376]{0,1:T(8,128)(2,1)} %add_convert_fusion.19), channel_id=1, source_target_pairs={{8,0},{12,4},{16,8},{20,12},{24,16},{28,20},{9,1},{13,5},{17,9},{2... | collective-permute-start | bytes 2113544 | tf_op jit(solution)/shard_map/ppermute | solution.py:38
  1071.9 47.0 %collective-permute-start.170 = (bf16[1376,256]{1,0:T(8,128)(2,1)S(1)}, bf16[1376,256]{1,0:T(8,128)(2,1)S(1)}, u32[]{:S(2)}, u32[]{:S(2)}) collective-permute-start(bf16[1376,256]{1,0:T(8,128)(2,1)S(1)} %collective-permute-done.169), channel_id=1, source_target_pairs={{8,0},{12,4},{16,8},{20,12},{9,1},{13,5},{17,9},{21,13},{10,2},{14... | collective-permute-start | bytes 2113544 | tf_op jit(solution)/shard_map/ppermute | solution.py:38
  1073.2 44.0 %collective-permute-start.143 = (bf16[256,1376]{0,1:T(8,128)(2,1)S(1)}, bf16[256,1376]{0,1:T(8,128)(2,1)S(1)}, u32[]{:S(2)}, u32[]{:S(2)}) collective-permute-start(bf16[256,1376]{0,1:T(8,128)(2,1)S(1)} %collective-permute-done.142), channel_id=1, source_target_pairs={{8,0},{12,4},{9,1},{13,5},{10,2},{14,6},{11,3},{15,7}} | collective-permute-start | bytes 2113544 | tf_op jit(solution)/shard_map/ppermute | solution.py:38
  1089.0 62.7 %collective-permute-start.168 = (bf16[1376,256]{1,0:T(8,128)(2,1)S(1)}, bf16[1376,256]{1,0:T(8,128)(2,1)S(1)}, u32[]{:S(2)}, u32[]{:S(2)}) collective-permute-start(bf16[1376,256]{1,0:T(8,128)(2,1)S(1)} %collective-permute-done.167), channel_id=1, source_target_pairs={{16,24},{20,28},{17,25},{21,29},{18,26},{22,30},{19,27},{23,31}} | collective-permute-start | bytes 2113544 | tf_op jit(solution)/shard_map/ppermute | solution.py:38
  (247 other events, 4772.5 us)

commit v2 on v1

v2 whole, which is shorter than its diff:
```python
import functools

import jax
import jax.numpy as jnp
from jax import lax
from jax.experimental import pallas as pl
from jax.experimental.pallas import tpu as pltpu
from jax.sharding import PartitionSpec as P

HEAD = 128
WINDOW = 1024
EPS = 1e-05
THETA = 10000.0
NEG = -1e30
LOG2E = 1.4426950408889634
CHUNKS = 2
BF16 = jnp.bfloat16
F32 = jnp.float32
VMEM_LIMIT = 48 * 1024 * 1024


def cost(us):
    return pl.CostEstimate(flops=0, bytes_accessed=int(us * 0.5 * 3.69e6), transcendentals=0)


class Order:
    def __init__(self):
        self.last = ()

    def gate(self, *arrays):
        tied = lax.optimization_barrier(tuple(arrays) + tuple(self.last))[: len(arrays)]
        return tied[0] if len(arrays) == 1 else tied

    def mark(self, *arrays):
        self.last = arrays


def tp_send(x, mask):
    peers = lax.axis_size("tp")
    return lax.ppermute(x, "tp", [(i, i ^ mask) for i in range(peers)])


def seq_shift(x, by):
    peers = lax.axis_size("seq")
    return lax.ppermute(x, "seq", [(i, i + by) for i in range(peers) if 0 <= i + by < peers])


def core_swap(x):
    peers = lax.axis_size("seq")
    return lax.ppermute(x, "seq", [(i, i ^ 1) for i in range(peers)])


def chip_pairs(x, chip_pairs_list):
    pairs = [(2 * a + k, 2 * b + k) for a, b in chip_pairs_list for k in range(2)]
    return lax.ppermute(x, "seq", pairs)


def between_spans(near, far, sign):
    core = lax.axis_index("seq") % 2
    return core_swap(pick(core if sign > 0 else 1 - core, near, far))


def total_over_all(x):
    peers, chips = lax.axis_size("tp"), lax.axis_size("seq") // 2
    mask = 1
    while mask < peers:
        x = x + tp_send(x, mask)
        mask *= 2
    x = x + core_swap(x)
    c = lax.axis_index("seq") // 2
    mid = chips // 2 - 1
    for i in range(mid):
        x = x + chip_pairs(x, [(i, i + 1), (chips - 1 - i, chips - 2 - i)])
    x = x + chip_pairs(x, [(mid, mid + 1), (mid + 1, mid)])
    for j in range(mid, 0, -1):
        moved = chip_pairs(x, [(j, j - 1), (chips - 1 - j, chips - j)])
        x = jnp.where((c == j - 1) | (c == chips - j), moved, x)
    return x


def tp_gather(x):
    peers = lax.axis_size("tp")
    if peers != 4:
        return [x] + [tp_send(x, m) for m in range(1, peers)]
    half = x.shape[0] // 2
    x1 = tp_send(x, 1)
    x2 = tp_send(x, 2)
    return [x, x1, x2, tp_send(x1[:half], 2), tp_send(x2[half:], 1)]


class TpReduce:
    def __init__(self, parts):
        self.parts = parts
        self.peers = lax.axis_size("tp")
        if self.peers == 4:
            self.a = tp_send(parts[3], 1)
            self.b = tp_send(parts[4], 2)

    def second(self, order):
        parts = self.parts
        if self.peers == 4:
            a, b = order.gate(self.a, self.b)
            x, y = reduce_second(parts[1], parts[2], a, b)
            order.mark(x, y)
            self.got = [tp_send(x, 1), tp_send(y, 2)]
        else:
            self.got = [tp_send(parts[m], m) for m in range(1, self.peers)]

    def terms(self):
        return [self.parts[0]] + self.got


class LineSum:
    def __init__(self, order, left, right, axis, parts=1):
        self.order, self.left, self.right, self.axis, self.parts = order, left, right, axis, parts
        s = lax.axis_index("seq")
        self.k, self.c = s % 2, s // 2
        self.chips = lax.axis_size("seq") // 2
        self.stage = [0] * parts
        self.moved = [None] * parts

    def begin(self):
        left, right = self.order.gate(self.left, self.right)
        (sent,) = outer(left, right, 1 - self.k, self.axis, 1)
        self.order.mark(sent)
        self.swapped = core_swap(sent)

    def own(self):
        left, right, swapped = self.order.gate(self.left, self.right, self.swapped)
        self.acc = list(outer(left, right, self.k, self.axis, self.parts, swapped))
        self.order.mark(self.acc[0])

    def launch(self, j=0):
        self.acc[j] = self.order.gate(self.acc[j])
        self.send(j)

    def send(self, j):
        c = self.chips
        mid = c // 2 - 1
        i = self.stage[j]
        if i < mid:
            pairs = [(i, i + 1), (c - 1 - i, c - 2 - i)]
        elif i == mid:
            pairs = [(mid, mid + 1), (mid + 1, mid)]
        else:
            n = 2 * mid + 1 - i
            pairs = [(n, n - 1), (c - 1 - n, c - n)]
        self.takers = [b for _, b in pairs]
        self.moved[j] = chip_pairs(self.acc[j], pairs)

    def step(self, j=0):
        acc, moved = self.order.gate(self.acc[j], self.moved[j])
        mid = self.chips // 2 - 1
        i = self.stage[j]
        if i <= mid:
            acc = fold(acc, moved)
        else:
            n = 2 * mid + 1 - i
            taker = (self.c == n - 1) | (self.c == self.chips - n)
            acc = pick(taker.astype(jnp.int32), acc, moved)
        self.acc[j] = acc
        self.order.mark(acc)
        self.stage[j] += 1
        if self.stage[j] < self.chips - 1:
            self.send(j)
        else:
            self.moved[j] = core_swap(acc)

    def rest(self):
        for j in range(self.parts):
            while self.stage[j] < self.chips - 1:
                self.step(j)

    def finish(self):
        self.rest()
        arrays = self.order.gate(*self.acc, *self.moved)
        out = unite(arrays[: self.parts], arrays[self.parts :], self.k, self.axis)
        self.order.mark(out)
        return out


def dot_tt(a, b):
    return lax.dot_general(a, b, (((1,), (1,)), ((), ())), preferred_element_type=F32)


def dot_nn(a, b):
    return lax.dot_general(a, b, (((1,), (0,)), ((), ())), preferred_element_type=F32)


def swap_lanes(x):
    half = x.shape[-1] // 2
    return jnp.concatenate([x[:, half:], x[:, :half]], axis=-1)


def params():
    return pltpu.CompilerParams(vmem_limit_bytes=VMEM_LIMIT)


def project_kernel(turns, norm, x_ref, cos_ref, sin_ref, gain_ref, *refs):
    n = len(turns)
    w_refs, out_ref = refs[:n], refs[-1]
    x = x_ref[...]
    if norm:
        v = x.astype(F32)
        inverse = lax.rsqrt(jnp.mean(v * v, axis=-1, keepdims=True) + EPS)
        x = (v * inverse * gain_ref[...]).astype(BF16)
        refs[-2][...] = x
    cos, sin = cos_ref[...], sin_ref[...]
    at = 0
    for turn, w_ref in zip(turns, w_refs):
        lin = dot_nn(x, w_ref[...])
        for h in range(lin.shape[1] // HEAD):
            part = lin[:, h * HEAD : (h + 1) * HEAD]
            if turn:
                part = part * cos + swap_lanes(part) * sin
            out_ref[:, at : at + HEAD] = part.astype(BF16)
            at += HEAD


def project(x, tables, gain, weights, turns, first, count, norm=False, normed=None):
    total, width = x.shape
    flat = sum(w.shape[1] for w in weights)
    block = 256 if count % 256 == 0 else 128
    skip = first // block
    rows_of = lambda n: pl.BlockSpec((block, n), lambda i: (i + skip, 0))
    out_specs = [pl.BlockSpec((block, flat), lambda i: (i, 0))]
    out_shape = [jax.ShapeDtypeStruct((count, flat), BF16)]
    if norm:
        out_specs.insert(0, rows_of(width))
        out_shape.insert(0, jax.ShapeDtypeStruct(x.shape, BF16))
    kept = [] if normed is None else [normed]
    return pl.pallas_call(
        functools.partial(project_kernel, turns, norm),
        grid=(count // block,),
        in_specs=[rows_of(width), rows_of(HEAD), rows_of(HEAD)]
        + [pl.BlockSpec((1, width), lambda i: (0, 0))]
        + [pl.BlockSpec(w.shape, lambda i: (0, 0)) for w in weights]
        + [pl.BlockSpec(memory_space=pl.ANY)] * len(kept),
        out_specs=out_specs,
        out_shape=out_shape,
        input_output_aliases={4 + len(weights): 0} if kept else {},
        compiler_params=params(),
        cost_estimate=cost(6),
        name="project",
    )(x, *tables, gain.reshape(1, width), *weights, *kept)


def attend_kernel(reach, low_ref, q_ref, *refs):
    k_refs, v_refs = refs[: reach + 1], refs[reach + 1 : 2 * reach + 2]
    out_ref, lse_ref = refs[-2:]
    span = q_ref.shape[0]
    c = HEAD ** (-0.5) * LOG2E
    q = q_ref[...]
    low = low_ref[...]
    key = lax.broadcasted_iota(jnp.int32, (span, span), 1)
    scores = []
    for d in range(reach + 1):
        s = dot_tt(q, k_refs[d][...])
        seen = key >= low + d * span
        if d == 0:
            seen = seen & (key <= lax.broadcasted_iota(jnp.int32, (span, span), 0))
        scores.append(jnp.where(seen, s, NEG))
    top = functools.reduce(jnp.maximum, scores)
    top = jnp.max(top, axis=-1, keepdims=True)
    total = jnp.zeros((span, span), F32)
    mixed = jnp.zeros((span, HEAD), F32)
    for d in range(reach + 1):
        e = jnp.exp2((scores[d] - top) * c)
        total = total + e
        mixed = mixed + dot_nn(e.astype(BF16), v_refs[d][...])
    total = jnp.sum(total, axis=-1, keepdims=True)
    out_ref[...] = (mixed / total).astype(BF16)
    lse = top * c + jnp.log2(total)
    lse_ref[...] = jnp.transpose(jnp.broadcast_to(lse, (span, 128)))[:1][None, None]


def attend(queries, spans, low_col, rows, first, before):
    flat = queries.shape[1]
    tokens = spans[0].shape[0]
    reach = len(spans) - 1
    heads = flat // HEAD
    span = tokens // rows
    head_spec = pl.BlockSpec((span, HEAD), lambda r, h: (r, h))
    value_spec = pl.BlockSpec((span, HEAD), lambda r, h: (r, heads + h))
    pairs = rows * heads * span * span * (reach + 1)
    return pl.pallas_call(
        functools.partial(attend_kernel, reach),
        grid=(rows, heads),
        in_specs=[
            pl.BlockSpec((span, 1), lambda r, h: (r + first, 0)),
            pl.BlockSpec((span, HEAD), lambda r, h: (r + first, h)),
        ]
        + [head_spec] * (reach + 1)
        + [value_spec] * (reach + 1)
        + [pl.BlockSpec(memory_space=pl.ANY)] * len(before),
        out_specs=[
            pl.BlockSpec((span, HEAD), lambda r, h: (r + first, h)),
            pl.BlockSpec((1, 1, 1, span), lambda r, h: (r, h, 0, 0)),
        ],
        out_shape=[
            jax.ShapeDtypeStruct(queries.shape, BF16),
            jax.ShapeDtypeStruct((rows, heads, 1, span), F32),
        ],
        input_output_aliases={2 + 2 * (reach + 1): 0} if before else {},
        compiler_params=params(),
        cost_estimate=cost(9),
        name="attend",
    )(low_col, queries, *spans, *spans, *before)


def query_back_kernel(reach, low_ref, cos_ref, sin_ref, lse_ref, q_ref, g_ref, o_ref, *refs):
    k_refs, v_refs = refs[: reach + 1], refs[reach + 1 : 2 * reach + 2]
    out_ref = refs[-1]
    span = q_ref.shape[0]
    c = HEAD ** (-0.5) * LOG2E
    q = q_ref[...]
    g = g_ref[...]
    low = low_ref[...]
    lse = jnp.transpose(jnp.broadcast_to(lse_ref[0, 0], (128, span)))[:, :1]
    delta = jnp.sum(g.astype(F32) * o_ref[...].astype(F32), axis=-1, keepdims=True)
    key = lax.broadcasted_iota(jnp.int32, (span, span), 1)
    grad = jnp.zeros((span, HEAD), F32)
    for d in range(reach + 1):
        keys = k_refs[d][...]
        s = dot_tt(q, keys)
        seen = key >= low + d * span
        if d == 0:
            seen = seen & (key <= lax.broadcasted_iota(jnp.int32, (span, span), 0))
        p = jnp.where(seen, jnp.exp2(s * c - lse), 0.0)
        dp = dot_tt(g, v_refs[d][...])
        ds = (p * (dp - delta)).astype(BF16)
        grad = grad + dot_nn(ds, keys)
    grad = grad * HEAD ** (-0.5)
    out_ref[...] = (grad * cos_ref[...] + swap_lanes(grad * sin_ref[...])).astype(BF16)


def query_back(queries, mixed_grad, mixed, spans, lse, low_col, tables, rows, first, before):
    flat = queries.shape[1]
    tokens = spans[0].shape[0]
    reach = len(spans) - 1
    heads = flat // HEAD
    span = tokens // rows
    head_spec = pl.BlockSpec((span, HEAD), lambda r, h: (r, h))
    value_spec = pl.BlockSpec((span, HEAD), lambda r, h: (r, heads + h))
    whole_spec = pl.BlockSpec((span, HEAD), lambda r, h: (r + first, h))
    table_spec = pl.BlockSpec((span, HEAD), lambda r, h: (r + first, 0))
    return pl.pallas_call(
        functools.partial(query_back_kernel, reach),
        grid=(rows, heads),
        in_specs=[
            pl.BlockSpec((span, 1), lambda r, h: (r + first, 0)),
            table_spec,
            table_spec,
            pl.BlockSpec((1, 1, 1, span), lambda r, h: (r, h, 0, 0)),
            whole_spec,
            whole_spec,
            whole_spec,
        ]
        + [head_spec] * (reach + 1)
        + [value_spec] * (reach + 1)
        + [pl.BlockSpec(memory_space=pl.ANY)] * len(before),
        out_specs=whole_spec,
        out_shape=jax.ShapeDtypeStruct(queries.shape, BF16),
        input_output_aliases={7 + 2 * (reach + 1): 0} if before else {},
        compiler_params=params(),
        cost_estimate=cost(10),
        name="query_back",
    )(low_col, *tables, lse, queries, mixed_grad, mixed, *spans, *spans, *before)


def key_back_kernel(reach, cos_ref, sin_ref, k_ref, v_ref, *refs):
    n = reach + 1
    stat_refs, q_refs, g_refs = [refs[i * n : (i + 1) * n] for i in range(3)]
    key_out, value_out, stats = refs[-3:]
    span = k_ref.shape[0]
    c = HEAD ** (-0.5) * LOG2E
    h = pl.program_id(1)

    @pl.when(h == 0)
    def _():
        for d in range(n):
            block = stat_refs[d][...].astype(F32)
            per_row = block.shape[1] // span
            for index in range(1 + 2 * (block.shape[1] // HEAD)):
                total = jnp.zeros((1, span), F32)
                for third in range(3):
                    v = 3 * index + third
                    row, column = v // per_row, v % per_row * span
                    total = total + block[row : row + 1, column : column + span]
                stats[d, index] = total

    keys = k_ref[...]
    values = v_ref[...]
    key = lax.broadcasted_iota(jnp.int32, (span, span), 0)
    key_grad = jnp.zeros((span, HEAD), F32)
    value_grad = jnp.zeros((span, HEAD), F32)
    for d in range(n):
        low = stats[d, 0].astype(jnp.int32) + d * span
        q = q_refs[d][...]
        g = g_refs[d][...]
        s = dot_tt(keys, q)
        seen = key >= low
        if d == 0:
            seen = seen & (key <= lax.broadcasted_iota(jnp.int32, (span, span), 1))
        p = jnp.where(seen, jnp.exp2(s * c - stats[d, 1 + 2 * h]), 0.0)
        value_grad = value_grad + dot_nn(p.astype(BF16), g)
        dp = dot_tt(values, g)
        ds = (p * (dp - stats[d, 2 + 2 * h])).astype(BF16)
        key_grad = key_grad + dot_nn(ds, q)
    key_grad = key_grad * HEAD ** (-0.5)
    key_out[...] = (key_grad * cos_ref[...] + swap_lanes(key_grad * sin_ref[...])).astype(BF16)
    value_out[...] = value_grad.astype(BF16)


def key_back(pair, queries, grads, tables, rows, first, before):
    total, flat = queries[0].shape
    tokens = pair.shape[0]
    n = len(queries)
    heads = flat // HEAD
    span = tokens // rows
    head_spec = pl.BlockSpec((span, HEAD), lambda r, h: (r, h))
    value_spec = pl.BlockSpec((span, HEAD), lambda r, h: (r, heads + h))
    whole_spec = pl.BlockSpec((span, HEAD), lambda r, h: (r + first, h))
    table_spec = pl.BlockSpec((span, HEAD), lambda r, h: (r + first, 0))
    stats_at = total // STAT_ROWS + first
    stat_spec = pl.BlockSpec((STAT_ROWS, flat), lambda r, h: (r + stats_at, 0))
    return pl.pallas_call(
        functools.partial(key_back_kernel, n - 1),
        grid=(rows, heads),
        in_specs=[table_spec, table_spec, head_spec, value_spec]
        + [stat_spec] * n
        + [whole_spec] * (2 * n)
        + [pl.BlockSpec(memory_space=pl.ANY)] * len(before),
        out_specs=[whole_spec, whole_spec],
        out_shape=[jax.ShapeDtypeStruct((total, flat), BF16)] * 2,
        input_output_aliases={4 + 3 * n + i: i for i in range(len(before))},
        scratch_shapes=[pltpu.VMEM((n, 1 + 2 * heads, 1, span), F32)],
        compiler_params=params(),
        cost_estimate=cost(11),
        name="key_back",
    )(*tables, pair, pair, *grads, *queries, *grads, *before)


def residual_kernel(parts, tok_ref, gain_ref, *refs):
    x_refs, w_refs = refs[:parts], refs[parts : 2 * parts]
    res_ref, normed_ref = refs[2 * parts :]
    n = pl.program_id(0)
    tile = w_refs[0].shape[1]
    total = tok_ref[...].astype(F32)
    for x_ref, w_ref in zip(x_refs, w_refs):
        total = total + dot_nn(x_ref[...], w_ref[...])
    res_ref[:, pl.ds(pl.multiple_of(n * tile, tile), tile)] = total

    @pl.when(n == pl.num_programs(0) - 1)
    def _():
        v = res_ref[...]
        inverse = lax.rsqrt(jnp.mean(v * v, axis=-1, keepdims=True) + EPS)
        normed_ref[...] = (v * inverse * gain_ref[...]).astype(BF16)


def residual_of(tok, gain, pieces, weights):
    count, width = tok.shape
    tile = 512
    depth = weights[0].shape[0]
    whole = pl.BlockSpec((count, width), lambda n: (0, 0))
    return pl.pallas_call(
        functools.partial(residual_kernel, len(pieces)),
        grid=(width // tile,),
        in_specs=[
            pl.BlockSpec((count, tile), lambda n: (0, n)),
            pl.BlockSpec((1, width), lambda n: (0, 0)),
        ]
        + [pl.BlockSpec((count, depth), lambda n: (0, 0)) for _ in pieces]
        + [pl.BlockSpec((depth, tile), lambda n: (0, n)) for _ in weights],
        out_specs=[whole, whole],
        out_shape=[
            jax.ShapeDtypeStruct((count, width), F32),
            jax.ShapeDtypeStruct((count, width), BF16),
        ],
        compiler_params=params(),
        cost_estimate=cost(5),
        name="residual",
    )(tok, gain.reshape(1, width), *pieces, *weights)


def act_grad_kernel(pieces, t_ref, w_ref, *refs):
    cot_refs = refs[:pieces]
    upstream_ref, out_ref = refs[pieces:]
    part = cot_refs[0].shape[0]

    @pl.when(pl.program_id(0) == 0)
    def _():
        for j, cot_ref in enumerate(cot_refs):
            upstream_ref[j * part : (j + 1) * part] = cot_ref[...]

    out_ref[...] = dot_tt(upstream_ref[...], w_ref[...])


def act_grad_of(cot, w_down, t, peers):
    count, width = cot.shape
    hidden = w_down.shape[0]
    tile = 256
    pieces = CHUNKS * peers
    part = count // pieces
    near = lambda i, m: pl.BlockSpec((part, width), lambda n, t: (i * peers + (t[0] ^ m), 0))
    return pl.pallas_call(
        functools.partial(act_grad_kernel, pieces),
        grid_spec=pltpu.PrefetchScalarGridSpec(
            num_scalar_prefetch=1,
            grid=(pl.cdiv(hidden, tile),),
            in_specs=[pl.BlockSpec((tile, width), lambda n, t: (n, 0))]
            + [near(i, m) for i in range(CHUNKS) for m in range(peers)],
            out_specs=[
                pl.BlockSpec((count, width), lambda n, t: (0, 0)),
                pl.BlockSpec((count, tile), lambda n, t: (0, n)),
            ],
        ),
        out_shape=[
            jax.ShapeDtypeStruct((count, width), BF16),
            jax.ShapeDtypeStruct((count, hidden), F32),
        ],
        compiler_params=params(),
        cost_estimate=cost(12),
        name="act_grad",
    )(t, w_down, *[cot] * pieces)


def split_kernel(part, t_ref, x_ref, *out_refs):
    for m, out_ref in enumerate(out_refs):
        at = pl.multiple_of((t_ref[0] ^ m) * part, part)
        out_ref[...] = x_ref[pl.ds(at, part), :]


def split_near(x, t, peers, chunk):
    part = x.shape[0] // (peers * CHUNKS)
    whole = lambda shape: pl.BlockSpec(shape, lambda n, t: (0, 0))
    piece = (part, x.shape[1])
    return pl.pallas_call(
        functools.partial(split_kernel, part),
        grid_spec=pltpu.PrefetchScalarGridSpec(
            num_scalar_prefetch=1,
            grid=(1,),
            in_specs=[pl.BlockSpec((part * peers, x.shape[1]), lambda n, t: (chunk, 0))],
            out_specs=[whole(piece)] * peers,
        ),
        out_shape=[jax.ShapeDtypeStruct(piece, x.dtype)] * peers,
        compiler_params=params(),
        cost_estimate=cost(1.5),
        name="split_near",
    )(t, x)


STAT_ROWS = 16


def thirds(x):
    high = x.astype(BF16)
    rest = x - high.astype(F32)
    mid = rest.astype(BF16)
    return high, mid, (rest - mid.astype(F32)).astype(BF16)


def join_kernel(part, peers, t_ref, low_ref, *refs):
    piece_refs, mixed_ref, lse_refs = refs[:peers], refs[peers], refs[peers + 1 : -1]
    out_ref = refs[-1]
    for m, x_ref in enumerate(piece_refs):
        for i in range(CHUNKS):
            at = pl.multiple_of((i * peers + (t_ref[0] ^ m)) * part, part)
            out_ref[pl.ds(at, part), :] = x_ref[i * part : (i + 1) * part]
    rows, span = low_ref.shape[0], low_ref.shape[2]
    heads = lse_refs[0].shape[1]
    count = rows * span
    chunk_rows = rows // CHUNKS
    out_ref[count:] = jnp.zeros((out_ref.shape[0] - count, out_ref.shape[1]), BF16)
    for r in range(rows):
        i = r // chunk_rows
        g = out_ref[r * span : (r + 1) * span].astype(F32)
        product = g * mixed_ref[r * span : (r + 1) * span].astype(F32)
        vectors = [low_ref[r]]
        for h in range(heads):
            vectors.append(lse_refs[i][r % chunk_rows, h])
            delta = jnp.sum(product[:, h * HEAD : (h + 1) * HEAD], axis=-1, keepdims=True)
            vectors.append(jnp.transpose(jnp.broadcast_to(delta, (span, 128)))[:1])
        per_row = out_ref.shape[1] // span
        for v, x in enumerate([third for x in vectors for third in thirds(x)]):
            row, column = count + r * STAT_ROWS + v // per_row, v % per_row * span
            out_ref[row : row + 1, column : column + span] = x


def join_true(pieces, mixed, lses, low, t):
    peers = len(pieces)
    rows, width = pieces[0].shape
    extra = low.shape[0] * STAT_ROWS
    whole = lambda x: pl.BlockSpec(x.shape, lambda n, t: (0,) * x.ndim)
    out = jax.ShapeDtypeStruct((peers * rows + extra, width), BF16)
    return pl.pallas_call(
        functools.partial(join_kernel, rows // CHUNKS, peers),
        grid_spec=pltpu.PrefetchScalarGridSpec(
            num_scalar_prefetch=1,
            grid=(1,),
            in_specs=[whole(x) for x in (low, *pieces, mixed, *lses)],
            out_specs=whole(out),
        ),
        out_shape=out,
        compiler_params=params(),
        cost_estimate=cost(4),
        name="join_true",
    )(t, low, *pieces, mixed, *lses)


def ffn_kernel(pieces, act_grad_ref, gate_ref, up_ref, *refs):
    x_refs = refs[:pieces]
    x_ref, activated_ref, gate_grad_ref, up_grad_ref = refs[-4:]

    @pl.when(pl.program_id(0) == 0)
    def _():
        at = 0
        for piece_ref in x_refs:
            x_ref[at : at + piece_ref.shape[0]] = piece_ref[...]
            at += piece_ref.shape[0]

    x = x_ref[...]
    gate_in = dot_tt(x, gate_ref[...])
    upward = dot_tt(x, up_ref[...])
    act_grad = act_grad_ref[...]
    sigmoid_gate = jax.nn.sigmoid(gate_in)
    swish_gate = gate_in * sigmoid_gate
    activated_ref[...] = (swish_gate * upward).astype(BF16)
    gate_grad_ref[...] = (
        act_grad * upward * (sigmoid_gate * (1.0 + gate_in * (1.0 - sigmoid_gate)))
    ).astype(BF16)
    up_grad_ref[...] = (act_grad * swish_gate).astype(BF16)


def ffn(x_pieces, act_grad, gate_t, up_t, chunk, before):
    hidden, width = gate_t.shape
    count = sum(x.shape[0] for x in x_pieces)
    tile = 384
    weight = pl.BlockSpec((tile, width), lambda n: (n, 0))
    block = pl.BlockSpec((count, tile), lambda n: (chunk, n))
    out = jax.ShapeDtypeStruct((CHUNKS * count, hidden), BF16)
    kept = [pl.BlockSpec(memory_space=pl.ANY)] * len(before)
    first = 3 + len(x_pieces)
    return pl.pallas_call(
        functools.partial(ffn_kernel, len(x_pieces)),
        grid=(pl.cdiv(hidden, tile),),
        in_specs=[block, weight, weight]
        + [pl.BlockSpec(x.shape, lambda n: (0, 0)) for x in x_pieces]
        + kept,
        out_specs=[pl.BlockSpec((count, width), lambda n: (chunk, 0))] + [block] * 3,
        out_shape=[jax.ShapeDtypeStruct((CHUNKS * count, width), BF16)] + [out] * 3,
        input_output_aliases={first + i: i for i in range(len(before))},
        compiler_params=params(),
        cost_estimate=cost(12),
        name="ffn",
    )(act_grad, gate_t, up_t, *x_pieces, *before)


def scatter_kernel(part, place_ref, x_ref, w_ref, out_ref):
    v = dot_nn(x_ref[...], w_ref[...]).astype(BF16)
    for j in range(x_ref.shape[0] // part):
        at = pl.multiple_of(place_ref[j] * part, part)
        out_ref[pl.ds(at, part), :] = v[j * part : (j + 1) * part]


def scattered_product(x, w, part, places):
    count, depth = x.shape
    width = w.shape[1]
    tile = 512
    return pl.pallas_call(
        functools.partial(scatter_kernel, part),
        grid_spec=pltpu.PrefetchScalarGridSpec(
            num_scalar_prefetch=1,
            grid=(width // tile,),
            in_specs=[
                pl.BlockSpec((count, depth), lambda n, place: (0, 0)),
                pl.BlockSpec((depth, tile), lambda n, place: (0, n)),
            ],
            out_specs=pl.BlockSpec((count, tile), lambda n, place: (0, n)),
        ),
        out_shape=jax.ShapeDtypeStruct((count, width), BF16),
        compiler_params=params(),
        cost_estimate=cost(10),
        name="ffn_part",
    )(places, x, w)


def input_back_kernel(terms, flip, part, peers, place_ref, *refs):
    g_refs, w_refs, out_refs = refs[:terms], refs[terms : 2 * terms], refs[2 * terms : -1]
    all_ref = refs[-1]
    product = dot_tt if flip else dot_nn
    total = product(g_refs[0][...], w_refs[0][...])
    for g_ref, w_ref in zip(g_refs[1:], w_refs[1:]):
        total = total + product(g_ref[...], w_ref[...])
    rows = []
    if not flip:
        for m in range(peers):
            for i in range(CHUNKS):
                at = (i * peers + m) * part
                rows.append(total[at : at + part].astype(BF16))
    else:
        all_ref[...] = total
        for m in range(peers):
            for i in range(CHUNKS):
                at = pl.multiple_of(place_ref[i * peers + m] * part, part)
                rows.append(all_ref[pl.ds(at, part), :].astype(BF16))
    for m in range(peers):
        own = rows[m * CHUNKS : (m + 1) * CHUNKS]
        if peers == 4 and m == 3:
            out_refs[3][...] = own[0]
            out_refs[4][...] = own[1]
        else:
            for i in range(CHUNKS):
                out_refs[m][i * part : (i + 1) * part] = own[i]


def input_back(grads, weights, flip, part, peers, places):
    count, depth = grads[0].shape
    width = weights[0].shape[0 if flip else 1]
    tile = 512
    terms = len(grads)
    sizes = [CHUNKS * part] * peers
    if peers == 4:
        sizes = [CHUNKS * part] * 3 + [part] * 2
    weight = (
        pl.BlockSpec((tile, depth), lambda n, place: (n, 0))
        if flip
        else pl.BlockSpec((depth, tile), lambda n, place: (0, n))
    )
    return pl.pallas_call(
        functools.partial(input_back_kernel, terms, flip, part, peers),
        grid_spec=pltpu.PrefetchScalarGridSpec(
            num_scalar_prefetch=1,
            grid=(width // tile,),
            in_specs=[pl.BlockSpec((count, depth), lambda n, place: (0, 0))] * terms
            + [weight] * terms,
            out_specs=[pl.BlockSpec((n_rows, tile), lambda n, place: (0, n)) for n_rows in sizes],
            scratch_shapes=[pltpu.VMEM((count, tile), F32)],
        ),
        out_shape=[jax.ShapeDtypeStruct((n_rows, width), BF16) for n_rows in sizes],
        compiler_params=params(),
        cost_estimate=cost(16),
        name="input_back",
    )(places, *grads, *weights)


def norm_back(term_refs, v, gain, base):
    c = term_refs[0][...].astype(F32)
    for term_ref in term_refs[1:]:
        c = c + term_ref[...].astype(F32)
    inverse = lax.rsqrt(jnp.mean(v * v, axis=-1, keepdims=True) + EPS)
    plain = v * inverse
    scaled = c * gain
    mean = jnp.mean(scaled * plain, axis=-1, keepdims=True)
    return base + inverse * (scaled - plain * mean), jnp.sum(c * plain, axis=0, keepdims=True)


def resid_back_kernel(terms, peers, gain_ref, *refs):
    term_refs = refs[:terms]
    res_refs = refs[terms : terms + CHUNKS]
    up_refs = refs[terms + CHUNKS : terms + 2 * CHUNKS]
    w_refs = refs[terms + 2 * CHUNKS : terms + 2 * CHUNKS + peers]
    grad_ref, low_ref, gain_out = refs[terms + 2 * CHUNKS + peers :][:3]
    g_refs = refs[terms + 2 * CHUNKS + peers + 3 :]
    n = pl.program_id(0)

    @pl.when(n == 0)
    def _():
        v = jnp.concatenate([ref[...] for ref in res_refs], axis=0)
        base = jnp.concatenate([ref[...] for ref in up_refs], axis=0).astype(F32)
        grad, gain_grad = norm_back(term_refs, v, gain_ref[...], base)
        grad_ref[...] = grad
        low_ref[...] = grad.astype(BF16)
        gain_out[...] = gain_grad

    low = low_ref[...]
    for m in range(peers):

        @pl.when(n == m)
        def _(m=m):
            g_refs[m][...] = dot_tt(low, w_refs[m][...]).astype(BF16)


def resid_back(terms, gain, residuals, upstream, weights):
    own, width = terms[0].shape
    part = own // CHUNKS
    peers = len(weights)
    depth = weights[0].shape[0]
    same = lambda shape: pl.BlockSpec(shape, lambda n: (0, 0))
    chunk_of = lambda i: pl.BlockSpec((part, width), lambda n: (i * peers, 0))
    return pl.pallas_call(
        functools.partial(resid_back_kernel, len(terms), peers),
        grid=(peers,),
        in_specs=[same((1, width))]
        + [same((own, width))] * len(terms)
        + [same((part, width))] * CHUNKS
        + [chunk_of(i) for i in range(CHUNKS)]
        + [same((depth, width))] * peers,
        out_specs=[same((own, width)), same((own, width)), same((1, width))]
        + [same((own, depth))] * peers,
        out_shape=[
            jax.ShapeDtypeStruct((own, width), F32),
            jax.ShapeDtypeStruct((own, width), BF16),
            jax.ShapeDtypeStruct((1, width), F32),
        ]
        + [jax.ShapeDtypeStruct((own, depth), BF16)] * peers,
        compiler_params=params(),
        cost_estimate=cost(11),
        name="resid_back",
    )(gain.reshape(1, width), *terms, *residuals, *[upstream] * CHUNKS, *weights)


def token_back_kernel(terms, t_ref, gain_ref, *refs):
    term_refs = refs[:terms]
    tok_refs = refs[terms : terms + CHUNKS]
    base_ref, out_ref, gain_out = refs[terms + CHUNKS :]
    v = jnp.concatenate([ref[...] for ref in tok_refs], axis=0).astype(F32)
    grad, gain_grad = norm_back(term_refs, v, gain_ref[...], base_ref[...])
    out_ref[...] = grad.astype(BF16)
    gain_out[...] = gain_grad


def token_back(terms, gain, tok, resid_grad, t, peers):
    own, width = terms[0].shape
    part = own // CHUNKS
    same = lambda shape: pl.BlockSpec(shape, lambda n, t: (0, 0))
    chunk_of = lambda i: pl.BlockSpec((part, width), lambda n, t: (i * peers + t[0], 0))
    return pl.pallas_call(
        functools.partial(token_back_kernel, len(terms)),
        grid_spec=pltpu.PrefetchScalarGridSpec(
            num_scalar_prefetch=1,
            grid=(1,),
            in_specs=[same((1, width))]
            + [same((own, width))] * len(terms)
            + [chunk_of(i) for i in range(CHUNKS)]
            + [same((own, width))],
            out_specs=[same((own, width)), same((1, width))],
        ),
        out_shape=[
            jax.ShapeDtypeStruct((own, width), BF16),
            jax.ShapeDtypeStruct((1, width), F32),
        ],
        compiler_params=params(),
        cost_estimate=cost(5),
        name="token_back",
    )(t, gain.reshape(1, width), *terms, *[tok] * CHUNKS, resid_grad)


def outer(left, right, k, axis, parts, add=None):
    if axis == 0:
        left = half_columns(left, k)
    else:
        right = half_columns(right, k)
    v = lax.dot_general(left, right, (((0,), (0,)), ((), ())), preferred_element_type=F32)
    if add is not None:
        v = v + add.astype(F32)
    v = v.astype(BF16)
    width = v.shape[1] // parts
    return [v[:, j * width : (j + 1) * width] for j in range(parts)]


def fold_kernel(a_ref, b_ref, out_ref):
    out_ref[...] = (a_ref[...].astype(F32) + b_ref[...].astype(F32)).astype(BF16)


def row_tile(rows):
    return 256 if rows % 256 == 0 else (352 if rows > 352 else rows)


def fold(a, b):
    rows, width = a.shape
    tile = row_tile(rows)
    block = pl.BlockSpec((tile, width), lambda i: (i, 0))
    return pl.pallas_call(
        fold_kernel,
        grid=(pl.cdiv(rows, tile),),
        in_specs=[block, block],
        out_specs=block,
        out_shape=jax.ShapeDtypeStruct(a.shape, BF16),
        input_output_aliases={0: 0},
        compiler_params=params(),
        cost_estimate=cost(1 + rows * width / 4e5),
        name="fold",
    )(a, b)


def pick_kernel(which_ref, a_ref, b_ref, out_ref):
    @pl.when(which_ref[0] == 0)
    def _():
        out_ref[...] = a_ref[...]

    @pl.when(which_ref[0] != 0)
    def _():
        out_ref[...] = b_ref[...]


def pick(which, a, b):
    rows, width = a.shape
    tile = row_tile(rows)
    return pl.pallas_call(
        pick_kernel,
        grid_spec=pltpu.PrefetchScalarGridSpec(
            num_scalar_prefetch=1,
            grid=(pl.cdiv(rows, tile),),
            in_specs=[
                pl.BlockSpec((tile, width), lambda i, which: (i * (1 - which[0]), 0)),
                pl.BlockSpec((tile, width), lambda i, which: (i * which[0], 0)),
            ],
            out_specs=pl.BlockSpec((tile, width), lambda i, which: (i, 0)),
        ),
        out_shape=jax.ShapeDtypeStruct(a.shape, a.dtype),
        compiler_params=params(),
        cost_estimate=cost(1 + rows * width / 5e5),
        name="pick",
    )(jnp.full((1,), which, jnp.int32), a, b)


def reduce_second_kernel(one_ref, two_ref, a_ref, b_ref, x_ref, y_ref):
    n = a_ref.shape[0]
    x_ref[:n] = one_ref[:n]
    x_ref[n:] = (one_ref[n:].astype(F32) + b_ref[...].astype(F32)).astype(BF16)
    y_ref[:n] = (two_ref[:n].astype(F32) + a_ref[...].astype(F32)).astype(BF16)
    y_ref[n:] = two_ref[n:]


def reduce_second(one, two, a, b):
    n, width = one.shape
    tile = 512
    whole = pl.BlockSpec((n, tile), lambda i: (0, i))
    half = pl.BlockSpec((n // 2, tile), lambda i: (0, i))
    return pl.pallas_call(
        reduce_second_kernel,
        grid=(width // tile,),
        in_specs=[whole, whole, half, half],
        out_specs=[whole, whole],
        out_shape=[jax.ShapeDtypeStruct(one.shape, BF16)] * 2,
        compiler_params=params(),
        cost_estimate=cost(2),
        name="reduce_second",
    )(one, two, a, b)


def reorder_kernel(x_ref, out_ref):
    out_ref[...] = x_ref[...]


def true_order(x, peers):
    count, width = x.shape
    part = count // (peers * CHUNKS)
    return pl.pallas_call(
        reorder_kernel,
        grid=(CHUNKS * peers,),
        in_specs=[
            pl.BlockSpec((part, width), lambda i: (i % peers * CHUNKS + i // peers, 0))
        ],
        out_specs=pl.BlockSpec((part, width), lambda i: (i, 0)),
        out_shape=jax.ShapeDtypeStruct(x.shape, x.dtype),
        compiler_params=params(),
        cost_estimate=cost(3),
        name="true_order",
    )(x)


def unite_kernel(parts, axis, k_ref, *refs):
    mine, theirs, out_ref = refs[:parts], refs[parts : 2 * parts], refs[-1]
    first = k_ref[0] == 0
    if axis == 0:
        first = first == (pl.program_id(0) < pl.num_programs(0) // 2)
        out_ref[...] = jnp.where(first, mine[0][...], theirs[0][...]).astype(F32)
        return
    width = mine[0].shape[1]
    for j in range(parts):
        a, b = mine[j][...].astype(F32), theirs[j][...].astype(F32)
        out_ref[:, j * width : (j + 1) * width] = jnp.where(first, a, b)
        at = (parts + j) * width
        out_ref[:, at : at + width] = jnp.where(first, b, a)


def unite(mine, theirs, k, axis):
    parts = len(mine)
    rows, width = mine[0].shape
    tile = 128 if rows % 128 else 256
    steps = pl.cdiv(rows, tile)
    if axis == 0:
        grid, shape = (2 * steps,), (2 * rows, width)
        half_at = lambda i, k: (i % steps, 0)
    else:
        grid, shape = (steps,), (rows, 2 * parts * width)
        half_at = lambda i, k: (i, 0)
    return pl.pallas_call(
        functools.partial(unite_kernel, parts, axis),
        grid_spec=pltpu.PrefetchScalarGridSpec(
            num_scalar_prefetch=1,
            grid=grid,
            in_specs=[pl.BlockSpec((tile, width), half_at)] * (2 * parts),
            out_specs=pl.BlockSpec((tile, shape[1]), lambda i, k: (i, 0)),
        ),
        out_shape=jax.ShapeDtypeStruct(shape, F32),
        compiler_params=params(),
        cost_estimate=cost(1.5 + shape[0] * shape[1] / 7e5),
        name="unite",
    )(jnp.full((1,), k, jnp.int32), *mine, *theirs)


def half_columns(x, k):
    width = x.shape[1] // 2
    return lax.dynamic_slice_in_dim(x, k * width, width, 1)


def per_device(
    tokens,
    positions,
    w_query,
    w_key,
    w_value,
    w_out,
    w_gate,
    w_up,
    w_down,
    gain_attn,
    gain_ffn,
    cotangent,
):
    rows, span, width = tokens.shape
    count = rows * span
    peers = lax.axis_size("tp")
    t = lax.axis_index("tp")
    reach = WINDOW // span
    flat = w_query.shape[1]
    heads = flat // HEAD
    hidden = w_gate.shape[1]
    chunk = count // CHUNKS
    chunk_rows = rows // CHUNKS
    part = chunk // peers
    order = Order()

    def piece(x, i, m):
        return lax.dynamic_slice_in_dim(x, i * chunk + (t ^ m) * part, part, 0)

    tok = tokens.reshape(count, width)
    cot = cotangent.reshape(count, width)

    t_arg = jnp.full((1,), t, jnp.int32)
    gate_t, up_t = w_gate.T, w_up.T
    out_rows = [w_out] + [tp_send(w_out, m) for m in range(1, min(peers, 3))]

    within = jnp.arange(span, dtype=jnp.int32)[None, :]
    low = jnp.maximum(within - positions, within - (WINDOW - 1))
    low_col = low.reshape(count, 1)
    low_rows = low.astype(F32).reshape(rows, 1, span)
    half_size = HEAD // 2
    freq = THETA ** (-jnp.arange(half_size, dtype=F32) / half_size)
    freq = jnp.concatenate([freq, freq])
    sign = jnp.concatenate([-jnp.ones(half_size, F32), jnp.ones(half_size, F32)])
    angles = positions.reshape(count, 1).astype(F32) * freq
    tables = (jnp.cos(angles), jnp.sin(angles) * sign)

    weights_kv = (w_key, w_value)
    normed_attn, pair_0 = project(
        tok, tables, gain_attn, weights_kv, (True, False), 0, chunk, True
    )
    order.mark(pair_0)
    far_0 = seq_shift(pair_0, 2)
    normed_attn, pair_1 = project(
        order.gate(tok), tables, gain_attn, weights_kv, (True, False), chunk, chunk, True,
        normed_attn,
    )
    order.mark(pair_1)
    pairs = [pair_0, pair_1]
    (queries,) = project(order.gate(normed_attn), tables, gain_attn, (w_query,), (True,), 0, count)
    order.mark(queries)
    q_far = seq_shift(queries, -2)

    def two_more(spans, far, sign):
        between = between_spans(spans[-1], far, sign)
        spans += [between, far]
        return seq_shift(far, 2 * sign) if len(spans) < reach + 1 else None

    spans = [[pair_0], [pair_1]]
    far_0 = order.gate(far_0)
    order.mark(far_0)
    next_0 = two_more(spans[0], far_0, 1)
    upstream_low, act_grad = act_grad_of(order.gate(cot), w_down, t_arg, peers)
    order.mark(act_grad)
    q_far = order.gate(q_far)
    order.mark(q_far)
    q_spans = [queries]
    q_next = two_more(q_spans, q_far, -1)

    if peers == 4:
        half = w_out.shape[0] // 2
        out_1, out_2 = order.gate(*out_rows[1:])
        order.mark(out_1, out_2)
        out_3 = (tp_send(out_1[:half], 2), tp_send(out_2[half:], 1))
    else:
        out_rows += [tp_send(w_out, m) for m in range(3, peers)]

    while next_0 is not None:
        far_0 = order.gate(next_0)
        order.mark(far_0)
        next_0 = two_more(spans[0], far_0, 1)
    far_1 = seq_shift(order.gate(pair_1), 2)

    def attention(i, before):
        gated = order.gate(*spans[i])
        mixed, lse = attend(queries, gated, low_col, chunk_rows, i * chunk_rows, before)
        order.mark(mixed)
        sent = split_near(mixed, t_arg, peers, i)
        order.mark(*sent)
        return mixed, lse, [sent[0]] + [tp_send(sent[m], m) for m in range(1, peers)]

    mixed_0, lse_0, pieces_0 = attention(0, ())

    far_1 = order.gate(far_1)
    order.mark(far_1)
    next_1 = two_more(spans[1], far_1, 1)

    if peers == 4:
        out_3 = jnp.concatenate(order.gate(*out_3), axis=0)
        order.mark(out_3)
        out_rows.append(out_3)

    def residual_step(i, pieces):
        pieces = order.gate(*pieces)
        residual, normed = residual_of(piece(tok, i, 0), gain_ffn, pieces, out_rows)
        order.mark(residual)
        return residual, tp_gather(normed)

    residual_0, gathered_0 = residual_step(0, pieces_0)

    while q_next is not None:
        q_far = order.gate(q_next)
        order.mark(q_far)
        q_next = two_more(q_spans, q_far, -1)
    while next_1 is not None:
        far_1 = order.gate(next_1)
        order.mark(far_1)
        next_1 = two_more(spans[1], far_1, 1)
    mixed, lse_1, pieces_1 = attention(1, (mixed_0,))

    def ffn_step(i, gathered, before):
        outs = ffn(order.gate(*gathered), act_grad, gate_t, up_t, i, before)
        order.mark(outs[0])
        return outs

    ffn_0 = ffn_step(0, gathered_0, ())
    residual_1, gathered_1 = residual_step(1, pieces_1)
    normed_ffn, activated, gate_grad, up_grad = ffn_step(1, gathered_1, tuple(ffn_0))

    sum_down = LineSum(order, activated, upstream_low, 1, 2)
    sum_gate = LineSum(order, gate_grad, normed_ffn, 1, 2)
    sum_up = LineSum(order, up_grad, normed_ffn, 1, 2)
    sum_down.begin()
    sum_gate.begin()
    sum_down.own()
    sum_down.launch(0)
    sum_down.launch(1)
    near = jnp.arange(CHUNKS * peers, dtype=jnp.int32)
    true = (jnp.arange(CHUNKS)[:, None] * peers + (t ^ jnp.arange(peers))).reshape(-1)
    true = true.astype(jnp.int32)
    gate_g, up_g = order.gate(gate_grad, up_grad)
    ffn_back = input_back([gate_g, up_g], [gate_t, up_t], False, part, peers, near)
    order.mark(*ffn_back)
    reduce_ffn = TpReduce(ffn_back)
    sum_gate.own()
    sum_down.step(0)
    sum_gate.launch(0)
    reduce_ffn.second(order)
    sum_up.begin()
    places = ((t ^ jnp.arange(peers)) * CHUNKS + jnp.arange(CHUNKS)[:, None]).reshape(-1)
    ffn_part = scattered_product(order.gate(activated), w_down, part, places.astype(jnp.int32))
    order.mark(ffn_part)
    sum_down.step(1)
    sum_gate.launch(1)

    terms = order.gate(*reduce_ffn.terms())
    resid_grad, resid_low, gain_ffn_grad, *grads_own = resid_back(
        terms, gain_ffn, [residual_0, residual_1], upstream_low, out_rows
    )
    order.mark(resid_low)
    grads_got = [grads_own[0]] + [tp_send(grads_own[m], m) for m in range(1, peers)]
    resid_all = lax.all_gather(resid_low, "tp", axis=0, tiled=True)
    sum_down.step(0)
    sum_up.own()

    mixed_grad = join_true(
        order.gate(*grads_got), mixed, [lse_0, lse_1], low_rows, t_arg
    )
    order.mark(mixed_grad)
    g_far = seq_shift(mixed_grad, -2)
    sum_gate.step(0)
    sum_up.launch(0)
    ffn_part = lax.optimization_barrier((ffn_part, resid_all))[0]
    out_sum = lax.psum_scatter(ffn_part, "tp", scatter_dimension=0, tiled=True)

    def query_step(i, lse_i, before):
        grad_g = order.gate(mixed_grad)
        query_grad = query_back(
            queries, grad_g, mixed, spans[i], lse_i, low_col, tables, chunk_rows,
            i * chunk_rows, before,
        )
        order.mark(query_grad)
        return query_grad

    query_grad = query_step(0, lse_0, ())
    sum_down.step(1)
    sum_gate.step(1)
    sum_up.launch(1)
    query_grad = query_step(1, lse_1, (query_grad,))
    sum_down.step(0)
    sum_query = LineSum(order, normed_attn, query_grad, 0)
    sum_query.begin()
    sum_gate.step(0)

    g_far = order.gate(g_far)
    order.mark(g_far)
    g_spans = [mixed_grad]
    g_next = two_more(g_spans, g_far, -1)
    sum_down.step(1)
    sum_query.own()
    sum_up.step(0)
    sum_query.launch()
    sum_gate.step(1)
    mixed_by_t = jnp.transpose(mixed.reshape(CHUNKS, peers, part, flat), (1, 0, 2, 3))
    sum_out = LineSum(order, mixed_by_t.reshape(count, flat), resid_all, 0)
    while g_next is not None:
        g_far = order.gate(g_next)
        order.mark(g_far)
        g_next = two_more(g_spans, g_far, -1)
    sum_out.begin()
    sum_up.step(1)
    sum_gate.step(0)
    sum_out.own()
    sum_out.launch()

    g_spans = list(order.gate(*g_spans))
    order.mark(*g_spans)
    key_value = ()
    for i in range(CHUNKS):
        g_first = order.gate(g_spans[0])
        key_value = key_back(
            pairs[i], q_spans, [g_first] + g_spans[1:], tables, chunk_rows, i * chunk_rows,
            tuple(key_value),
        )
        order.mark(*key_value)
        if i == 0:
            sum_up.step(0)
            sum_query.step()
    key_grad, value_grad = key_value
    sum_key = LineSum(order, normed_attn, key_grad, 0)
    sum_value = LineSum(order, normed_attn, value_grad, 0)
    sum_key.begin()
    sum_value.begin()
    sum_key.own()
    sum_key.launch()
    sum_gate.step(1)

    key_g, value_g, query_g = order.gate(key_grad, value_grad, query_grad)
    attn_back = input_back(
        [query_g, key_g, value_g], [w_query, w_key, w_value], True, part, peers, true
    )
    order.mark(*attn_back)
    reduce_attn = TpReduce(attn_back)
    sum_value.own()
    sum_value.launch()
    sum_up.step(1)
    sum_out.step()
    reduce_attn.second(order)
    full_down = sum_down.finish()
    sum_up.step(0)
    sum_query.step()
    sum_key.step()
    full_gate = sum_gate.finish()

    terms = order.gate(*reduce_attn.terms())
    token_grad, gain_attn_grad = token_back(terms, gain_attn, tok, resid_grad, t_arg, peers)
    order.mark(token_grad)
    residual = jnp.concatenate([residual_0, residual_1], axis=0)
    output = (residual + out_sum.astype(F32)).astype(BF16)

    def gathered(own):
        whole = lax.all_gather(own, "tp", axis=0, tiled=True)
        return true_order(whole, peers).reshape(rows, span, width)

    token_grad = gathered(token_grad)
    output = gathered(output)
    gain_grads = total_over_all(jnp.concatenate([gain_attn_grad, gain_ffn_grad], axis=0))

    sum_value.step()
    sum_up.step(1)
    sum_out.step()
    sum_query.step()
    sum_key.step()
    full_up = sum_up.finish()
    sum_value.step()
    sum_out.step()
    full_query = sum_query.finish()
    sum_key.step()
    full_out = sum_out.finish()
    sum_value.step()
    full_key = sum_key.finish()
    full_value = sum_value.finish()
    return (
        output,
        token_grad,
        full_query,
        full_key,
        full_value,
        full_out,
        full_gate.T,
        full_up.T,
        full_down,
        gain_grads[0],
        gain_grads[1],
    )


def solution(mesh):
    return jax.shard_map(
        per_device,
        mesh=mesh,
        in_specs=(
            P(None, "seq", None),
            P(None, "seq"),
            P(None, "tp"),
            P(None, "tp"),
            P(None, "tp"),
            P("tp", None),
            P(None, "tp"),
            P(None, "tp"),
            P("tp", None),
            P(),
            P(),
            P(None, "seq", None),
        ),
        out_specs=(
            P(None, "seq", None),
            P(None, "seq", None),
            P(None, "tp"),
            P(None, "tp"),
            P(None, "tp"),
            P("tp", None),
            P(None, "tp"),
            P(None, "tp"),
            P("tp", None),
            P(),
            P(),
        ),
        check_vma=False,
    )
```

time: 1230 us -> 879 us (0.71)
  Pallas kernels: 63.1 us -> 328 us
  waiting for transfers between devices: 473 us -> 217 us
  starting transfers between devices: 313 us -> 178 us
  other arithmetic: 107 us -> 6.75 us
  matrix products: 151 us -> 60.5 us
  blocking collectives: 40.5 us -> 0 us
    pallas_call x0 -> x65, Pallas kernels: none -> 261 us  [the longest x20 55.8 us: fold(): pl.pallas_call(fold_kernel, grid=(pl.cdiv(rows, tile),), in_specs=[block,...]
    ppermute x51 -> x31, waiting for transfers between devices: 152 us -> 49.4 us  [tp_send(): return lax.ppermute(x, 'tp', [(i, i ^ mask) for i in range(peers)])]
    ppermute x18 -> x8, waiting for transfers between devices: 124 us -> 24.2 us  [seq_shift(): lax.ppermute(x, 'seq', [(i, i + by) for i in range(peers) if 0 <= i + by...]
    ppermute x84 -> x33, starting transfers between devices: 206 us -> 113 us  [chip_pairs(): return lax.ppermute(x, 'seq', pairs)]
    dot_general x34 -> x14, matrix products: 151 us -> 60.5 us  [outer(): lax.dot_general(left, right, (((0,), (0,)), ((), ())), preferred_element_...]
    ppermute x84 -> x33, waiting for transfers between devices: 197 us -> 129 us  [chip_pairs(): return lax.ppermute(x, 'seq', pairs)]
    psum x1 -> x0, blocking collectives: 40.5 us -> none  [per_device(): lax.psum(jnp.stack([gain_attn_grad, gain_ffn_grad]), ('seq', 'tp'))]
    concatenate x11 -> x2, other arithmetic: 29.2 us -> 0.1 us  [the longest x1 0.08 us: per_device(): freq = jnp.concatenate([freq, freq])]
  transfers between devices with their start and end apart: 173 -> 102, of which waited for: 60 -> 32; matrix products, arithmetic and copies ran while one was open for 17% -> 9% of each run, Pallas kernels for 5% -> 34%
where the time goes in v2:
time: 879 us; the launch traced here: 867 us
  Pallas kernels  328 us (37%)
  waiting for transfers between devices  217 us (25%)
  starting transfers between devices  178 us (20%)
  matrix products  60.5 us (7%)
  local copies, waits for them, and re-layouts  60.3 us (7%)
  between operations  16 us (2%)
    ppermute x33, waiting for transfers between devices, chip_pairs(): return lax.ppermute(x, 'seq', pairs)  129 us
    ppermute x33, starting transfers between devices, chip_pairs(): return lax.ppermute(x, 'seq', pairs)  113 us
    dot_general x14, matrix products, outer(): lax.dot_general(left, right, (((0,), (0,)), ((), ())), preferred_element_...  60.5 us
    pallas_call x20, Pallas kernels, fold(): pl.pallas_call(fold_kernel, grid=(pl.cdiv(rows, tile),), in_specs=[block,...  55.8 us
    ppermute x31, waiting for transfers between devices, tp_send(): return lax.ppermute(x, 'tp', [(i, i ^ mask) for i in range(peers)])  49.4 us
    unnamed x206, local copies, waits for them, and re-layouts  44.5 us
    pallas_call x7, Pallas kernels, unite(): pl.pallas_call(functools.partial(unite_kernel, parts, axis), grid_spec=pl...  37.9 us
    ppermute x31, starting transfers between devices, tp_send(): return lax.ppermute(x, 'tp', [(i, i ^ mask) for i in range(peers)])  36.2 us
  transfers between devices with their start and end apart: 102, of which 32 were waited for; matrix products, arithmetic and copies ran while one was open for 9% of the time, Pallas kernels for 34%

profile of v2, /device:TPU:0, one launch (start us, length us, event | category | flops | bytes accessed | tf_op | source)
XLA Modules:
  0.0 867.4 jit_solution(8445638077725246395)
XLA Ops:
  38.8 9.4 %collective-permute-done.b_ref.a_ref.refs_2_.refs_7_ = bf16[512,1024]{1,0:T(8,128)(2,1)S(1)} collective-permute-done((bf16[512,1024]{1,0:T(8,128)(2,1)S(1)}, bf16[512,1024]{1,0:T(8,128)(2,1)S(1)}, u32[]{:S(2)}, u32[]{:S(2)}) %collective-permute-start) | collective-permute-done | bytes 1048608 | tf_op jit(solution)/shard_map/ppermute | solution.py:45
  53.5 12.0 %act_grad.1 = (bf16[1024,2048]{1,0:T(8,128)(2,1)S(1)}, f32[1024,1376]{1,0:T(8,128)}) custom-call(s32[1]{0:T(128)} %bitcast.2.t_ref, bf16[1376,2048]{1,0:T(8,128)(2,1)} %w_ref.3, bf16[1024,2048]{1,0:T(8,128)(2,1)} %bitcast.54, bf16[1024,2048]{1,0:T(8,128)(2,1)} %bitcast.55, bf16[1024,2048]{1,0:T(8,128)(2,1)} %bitcast.56, bf16[1024,2048]{1,0:T(8,128)(2,1)} %bitcast.57, ...), custom_call_target="tpu_custom_call" | custom-call | bytes 22140000 | tf_op jit(solution)/shard_map/act_grad/pallas_call | solution.py:506
  92.4 9.5 %attend.2 = (bf16[1024,512]{1,0:T(8,128)(2,1)S(1)}, f32[2,4,1,256]{3,2,1,0:T(1,128)S(1)}) custom-call(s32[1024,1]{1,0:T(8,128)S(1)} %bitcast.43, bf16[1024,512]{1,0:T(8,128)(2,1)S(1)} %project.5.q_ref.a_ref.refs_5_, bf16[512,1024]{1,0:T(8,128)(2,1)S(1)} %get-tuple-element.278.a_ref.refs_0_.refs_5_.k_ref.v_ref, ...), custom_call_target="tpu_custom_call" | custom-call | bytes 16605000 | tf_op jit(solution)/shard_map/attend/pallas_call | solution.py:286
  134.7 11.7 %collective-permute-done.20.refs_1_ = bf16[128,2048]{1,0:T(8,128)(2,1)S(1)} collective-permute-done((bf16[128,2048]{1,0:T(8,128)(2,1)S(1)}, bf16[128,2048]{1,0:T(8,128)(2,1)S(1)}, u32[]{:S(2)}, u32[]{:S(2)}) %collective-permute-start.20) | collective-permute-done | bytes 524320 | tf_op jit(solution)/shard_map/ppermute | solution.py:40
  150.2 9.5 %attend.3 = (bf16[1024,512]{1,0:T(8,128)(2,1)S(1)}, f32[2,4,1,256]{3,2,1,0:T(1,128)S(1)}) custom-call(s32[1024,1]{1,0:T(8,128)S(1)} %bitcast.44, bf16[1024,512]{1,0:T(8,128)(2,1)S(1)} %project.5.q_ref.a_ref.refs_5_, bf16[512,1024]{1,0:T(8,128)(2,1)} %get-tuple-element.300.a_ref.refs_0_.refs_5_.k_ref.v_ref, ...), custom_call_target="tpu_custom_call", output_to_operand_aliasing={{0}: (12, {})} | custom-call | bytes 16605000 | tf_op jit(solution)/shard_map/attend/pallas_call | solution.py:286
  163.3 13.3 %ffn.2 = (bf16[1024,2048]{1,0:T(8,128)(2,1)}, bf16[1024,1376]{1,0:T(8,128)(2,1)S(1)}, bf16[1024,1376]{1,0:T(8,128)(2,1)}, bf16[1024,1376]{1,0:T(8,128)(2,1)}) custom-call(f32[1024,1376]{1,0:T(8,128)} %get-tuple-element.273.act_grad_ref, bf16[1376,2048]{1,0:T(8,128)(2,1)} %bitcast.67, bf16[1376,2048]{1,0:T(8,128)(2,1)} %bitcast.70, ...), custom_call_target="tpu_custom_call" | custom-call | bytes 22140000 | tf_op jit(solution)/shard_map/ffn/pallas_call | solution.py:644
  185.5 10.4 %collective-permute-done.24.refs_1_ = bf16[128,2048]{1,0:T(8,128)(2,1)S(1)} collective-permute-done((bf16[128,2048]{1,0:T(8,128)(2,1)S(1)}, bf16[128,2048]{1,0:T(8,128)(2,1)S(1)}, u32[]{:S(2)}, u32[]{:S(2)}) %collective-permute-start.24) | collective-permute-done | bytes 524320 | tf_op jit(solution)/shard_map/ppermute | solution.py:40
  207.5 13.2 %ffn.3 = (bf16[1024,2048]{1,0:T(8,128)(2,1)}, bf16[1024,1376]{1,0:T(8,128)(2,1)S(1)}, bf16[1024,1376]{1,0:T(8,128)(2,1)}, bf16[1024,1376]{1,0:T(8,128)(2,1)}) custom-call(f32[1024,1376]{1,0:T(8,128)} %get-tuple-element.273.act_grad_ref, bf16[1376,2048]{1,0:T(8,128)(2,1)} %bitcast.68, ...), custom_call_target="tpu_custom_call", output_to_operand_aliasing={{0}: (8, {}), {1}: (9, {}), {2}: (10, {}), {3}: (11, {})} | custom-call | bytes 22140000 | tf_op jit(solution)/shard_map/ffn/pallas_call | solution.py:644
  243.4 18.8 %input_back.2 = (bf16[256,2048]{1,0:T(8,128)(2,1)S(1)}, bf16[256,2048]{1,0:T(8,128)(2,1)S(1)}, bf16[256,2048]{1,0:T(8,128)(2,1)S(1)}, bf16[128,2048]{1,0:T(8,128)(2,1)S(1)}, bf16[128,2048]{1,0:T(8,128)(2,1)S(1)}) custom-call(s32[8]{0:T(128)S(1)} %iota.34.place_ref, bf16[1024,1376]{1,0:T(8,128)(2,1)} %get-tuple-element.351.refs_0_, ...), custom_call_target="tpu_custom_call" | custom-call | bytes 29520000 | tf_op jit(solution)/shard_map/input_back/pallas_call | solution.py:730
  283.1 7.3 convolution_convert_fusion
  290.4 10.0 %ffn_part.1 = bf16[1024,2048]{1,0:T(8,128)(2,1)} custom-call(s32[8]{0:T(128)S(1)} %add.140.place_ref, bf16[1024,1376]{1,0:T(8,128)(2,1)S(1)} %copy-done.33, bf16[1376,2048]{1,0:T(8,128)(2,1)} %w_ref.3), custom_call_target="tpu_custom_call" | custom-call | bytes 18450000 | tf_op jit(solution)/shard_map/ffn_part/pallas_call | solution.py:670
  308.0 12.1 %resid_back.1 = (f32[256,2048]{1,0:T(8,128)}, bf16[256,2048]{1,0:T(8,128)(2,1)}, f32[1,2048]{1,0:T(1,128)S(1)}, bf16[256,512]{1,0:T(8,128)(2,1)S(1)}, bf16[256,5...) custom-call(f32[1,2048]{1,0:T(1,128)S(1)} %bitcast.53, ...), custom_call_target="tpu_custom_call" | custom-call | bytes 20295000 | tf_op jit(solution)/shard_map/resid_back/pallas_call | solution.py:791
  365.8 12.3 %all-gather.4.cloned.1.call-done = bf16[1024,2048]{1,0:T(8,128)(2,1)} async-done(((bf16[256,2048]{1,0:T(8,128)(2,1)}), bf16[1024,2048]{1,0:T(8,128)(2,1)}) %all-gather.4.cloned.1.call-update) | async-done | bytes 4194320 | tf_op jit(solution)/shard_map/all_gather | solution.py:1182
  382.5 11.7 %query_back.2.refs_10_ = bf16[1024,512]{1,0:T(8,128)(2,1)S(1)} custom-call(s32[1024,1]{1,0:T(8,128)S(1)} %bitcast.45, f32[1024,128]{1,0:T(8,128)S(1)} %copy-done.14, f32[1024,128]{1,0:T(8,128)S(1)} %copy-done.10, f32[2,4,1,256]{3,2,1,0:T(1,128)S(1)} %get-tuple-element.384.refs_5_.lse_ref, bf16[1024,512]{1,0:T(8,128)(2,1)S(1)} %project.5.q_ref.a_ref.refs_5_, ...), custom_call_target="tpu_custom_call" | custom-call | bytes 18450000 | tf_op jit(solution)/shard_map/query_back/pallas_call | solution.py:347
  404.5 11.7 %query_back.3.refs_0_ = bf16[1024,512]{1,0:T(8,128)(2,1)S(1)} custom-call(s32[1024,1]{1,0:T(8,128)S(1)} %bitcast.46, f32[1024,128]{1,0:T(8,128)S(1)} %copy-done.15, f32[1024,128]{1,0:T(8,128)S(1)} %copy-done.11, f32[2,4,1,256]{3,2,1,0:T(1,128)S(1)} %get-tuple-element.385.refs_6_.lse_ref, ...), custom_call_target="tpu_custom_call", output_to_operand_aliasing={{}: (17, {})} | custom-call | bytes 18450000 | tf_op jit(solution)/shard_map/query_back/pallas_call | solution.py:347
  422.1 23.5 %collective-permute-start.50 = (bf16[1376,512]{1,0:T(8,128)(2,1)}, bf16[1376,512]{1,0:T(8,128)(2,1)}, u32[]{:S(2)}, u32[]{:S(2)}) collective-permute-start(bf16[1376,512]{1,0:T(8,128)(2,1)} %get-tuple-element.409.a_ref), channel_id=1, source_target_pairs={{0,8},{4,12},{24,16},{28,20},{1,9},{5,13},{25,17},{29,21},{2,10},{... | collective-permute-start | bytes 4227080 | tf_op jit(solution)/shard_map/ppermute | solution.py:55
  456.3 13.7 %collective-permute-done.52.b_ref = bf16[1376,512]{1,0:T(8,128)(2,1)} collective-permute-done((bf16[1376,512]{1,0:T(8,128)(2,1)}, bf16[1376,512]{1,0:T(8,128)(2,1)}, u32[]{:S(2)}, u32[]{:S(2)}) %collective-permute-start.52) | collective-permute-done | bytes 1409056 | tf_op jit(solution)/shard_map/ppermute | solution.py:55
  511.2 8.5 collective-permute-done.55.b_ref
  520.8 25.0 %collective-permute-start.57 = (bf16[1024,512]{1,0:T(8,128)(2,1)}, bf16[1024,512]{1,0:T(8,128)(2,1)}, u32[]{:S(2)}, u32[]{:S(2)}) collective-permute-start(bf16[1024,512]{1,0:T(8,128)(2,1)} %add_convert_fusion.5.a_ref), channel_id=1, source_target_pairs={{0,8},{4,12},{24,16},{28,20},{1,9},{5,13},{25,17},{29,21},{2,10},{... | collective-permute-start | bytes 3145736 | tf_op jit(solution)/shard_map/ppermute | solution.py:55
  556.7 12.7 %key_back.2 = (bf16[1024,512]{1,0:T(8,128)(2,1)S(1)}, bf16[1024,512]{1,0:T(8,128)(2,1)S(1)}) custom-call(f32[1024,128]{1,0:T(8,128)S(1)} %copy-done.16, f32[1024,128]{1,0:T(8,128)S(1)} %copy-done.12, bf16[512,1024]{1,0:T(8,128)(2,1)S(1)} %get-tuple-element.278.a_ref.refs_0_.refs_5_.k_ref.v_ref, ...), custom_call_target="tpu_custom_call" | custom-call | bytes 20295000 | tf_op jit(solution)/shard_map/key_back/pallas_call | solution.py:427
  576.9 12.6 %key_back.3 = (bf16[1024,512]{1,0:T(8,128)(2,1)S(1)}, bf16[1024,512]{1,0:T(8,128)(2,1)S(1)}) custom-call(f32[1024,128]{1,0:T(8,128)S(1)} %copy-done.16, f32[1024,128]{1,0:T(8,128)S(1)} %copy-done.12, bf16[512,1024]{1,0:T(8,128)(2,1)} %get-tuple-element.300.a_ref.refs_0_.refs_5_.k_ref.v_ref, ...), custom_call_target="tpu_custom_call", output_to_operand_aliasing={{0}: (19, {}), {1}: (20, {})} | custom-call | bytes 20295000 | tf_op jit(solution)/shard_map/key_back/pallas_call | solution.py:427
  601.4 6.7 collective-permute-start.65
  615.4 11.0 %input_back.3 = (bf16[256,2048]{1,0:T(8,128)(2,1)S(1)}, bf16[256,2048]{1,0:T(8,128)(2,1)S(1)}, bf16[256,2048]{1,0:T(8,128)(2,1)S(1)}, bf16[128,2048]{1,0:T(8,128)(2,1)S(1)}, bf16[128,2048]{1,0:T(8,128)(2,1)S(1)}) custom-call(s32[8]{0:T(128)S(1)} %add.149.place_ref, bf16[1024,512]{1,0:T(8,128)(2,1)S(1)} %copy-done.43, bf16[1024,512]{1,0:T(8,128)(2,1)} %copy-done.56, ...), custom_call_target="tpu_custom_call" | custom-call | bytes 29520000 | tf_op jit(solution)/shard_map/input_back/pallas_call | solution.py:730
  630.1 11.3 %collective-permute-done.63.a_ref = bf16[128,2048]{1,0:T(8,128)(2,1)S(1)} collective-permute-done((bf16[128,2048]{1,0:T(8,128)(2,1)S(1)}, bf16[128,2048]{1,0:T(8,128)(2,1)S(1)}, u32[]{:S(2)}, u32[]{:S(2)}) %collective-permute-start.63) | collective-permute-done | bytes 524320 | tf_op jit(solution)/shard_map/ppermute | solution.py:40
  661.4 9.2 %unite.7 = f32[1376,2048]{1,0:T(8,128)} custom-call(s32[1]{0:T(128)} %bitcast.4.which_ref.k_ref, bf16[1376,512]{1,0:T(8,128)(2,1)S(1)} %copy-done.47, bf16[1376,512]{1,0:T(8,128)(2,1)} %pick.24.refs_1_, bf16[1376,512]{1,0:T(8,128)(2,1)S(1)} %copy-done.64, bf16[1376,512]{1,0:T(8,128)(2,1)} %collective-permute-done.76.refs_3_), custom_call_target="tpu_custom_call" | custom-call | bytes 10195069 | tf_op jit(solution)/shard_map/unite/pallas_call | solution.py:990
  679.4 9.6 %unite.8 = f32[1376,2048]{1,0:T(8,128)} custom-call(s32[1]{0:T(128)} %bitcast.4.which_ref.k_ref, bf16[1376,512]{1,0:T(8,128)(2,1)S(1)} %copy-done.49, bf16[1376,512]{1,0:T(8,128)(2,1)S(1)} %pick.29.refs_1_, bf16[1376,512]{1,0:T(8,128)(2,1)} %collective-permute-done.70.refs_2_, bf16[1376,512]{1,0:T(8,128)(2,1)} %collective-permute-done.71.refs_3_), custom_call_target="tpu_custom_call" | custom-call | bytes 10195069 | tf_op jit(solution)/shard_map/unite/pallas_call | solution.py:990
  705.4 20.1 %collective-permute-done.80.b_ref = bf16[1024,512]{1,0:T(8,128)(2,1)S(1)} collective-permute-done((bf16[1024,512]{1,0:T(8,128)(2,1)}, bf16[1024,512]{1,0:T(8,128)(2,1)S(1)}, u32[]{:S(2)}, u32[]{:S(2)}) %collective-permute-start.80) | collective-permute-done | bytes 1048608 | tf_op jit(solution)/shard_map/ppermute | solution.py:55
  735.9 18.2 %collective-permute-done.77.b_ref = bf16[1024,512]{1,0:T(8,128)(2,1)S(1)} collective-permute-done((bf16[1024,512]{1,0:T(8,128)(2,1)}, bf16[1024,512]{1,0:T(8,128)(2,1)S(1)}, u32[]{:S(2)}, u32[]{:S(2)}) %collective-permute-start.77) | collective-permute-done | bytes 1048608 | tf_op jit(solution)/shard_map/ppermute | solution.py:55
  765.2 16.9 %collective-permute-done.82.b_ref = bf16[256,2048]{1,0:T(8,128)(2,1)} collective-permute-done((bf16[256,2048]{1,0:T(8,128)(2,1)S(1)}, bf16[256,2048]{1,0:T(8,128)(2,1)}, u32[]{:S(2)}, u32[]{:S(2)}) %collective-permute-start.82) | collective-permute-done | bytes 1048608 | tf_op jit(solution)/shard_map/ppermute | solution.py:55
  793.7 10.9 %collective-permute-done.87.b_ref = bf16[1024,512]{1,0:T(8,128)(2,1)S(1)} collective-permute-done((bf16[1024,512]{1,0:T(8,128)(2,1)S(1)}, bf16[1024,512]{1,0:T(8,128)(2,1)S(1)}, u32[]{:S(2)}, u32[]{:S(2)}) %collective-permute-start.87) | collective-permute-done | bytes 1048608 | tf_op jit(solution)/shard_map/ppermute | solution.py:55
  809.2 15.6 %collective-permute-done.89.b_ref = bf16[1024,512]{1,0:T(8,128)(2,1)S(1)} collective-permute-done((bf16[1024,512]{1,0:T(8,128)(2,1)S(1)}, bf16[1024,512]{1,0:T(8,128)(2,1)S(1)}, u32[]{:S(2)}, u32[]{:S(2)}) %collective-permute-start.89) | collective-permute-done | bytes 1048608 | tf_op jit(solution)/shard_map/ppermute | solution.py:55
  832.6 8.9 %collective-permute-done.97 = f32[2,2048]{1,0:T(2,128)S(1)} collective-permute-done((f32[2,2048]{1,0:T(2,128)S(1)}, f32[2,2048]{1,0:T(2,128)S(1)}, u32[]{:S(2)}, u32[]{:S(2)}) %collective-permute-start.97) | collective-permute-done | bytes 16416 | tf_op jit(solution)/shard_map/ppermute | solution.py:55
  (502 shorter events, 444.0 us)
Async XLA Ops:
  7.2 370.9 %all-gather.4.cloned.1.call-start = ((), (), s32[]{:S(2)}) async-start(), calls=%async_computation.1 | async-start | bytes 5242880 | tf_op jit(solution)/shard_map/all_gather | solution.py:1182
  7.2 61.4 %collective-permute-start.3 = (bf16[512,2048]{1,0:T(8,128)(2,1)}, bf16[512,2048]{1,0:T(8,128)(2,1)}, u32[]{:S(2)}, u32[]{:S(2)}) collective-permute-start(bf16[512,2048]{1,0:T(8,128)(2,1)} %refs_7_.1), channel_id=1, source_target_pairs={{0,1},{1,0},{2,3},{3,2},{4,5},{5,4},{6,7},{7,6},{8,9},{9,8},{10,11... | collective-permute-start | bytes 6291464 | tf_op jit(solution)/shard_map/ppermute | solution.py:40
  10.2 58.4 %collective-permute-start.4 = (bf16[512,2048]{1,0:T(8,128)(2,1)}, bf16[512,2048]{1,0:T(8,128)(2,1)}, u32[]{:S(2)}, u32[]{:S(2)}) collective-permute-start(bf16[512,2048]{1,0:T(8,128)(2,1)} %refs_7_.1), channel_id=1, source_target_pairs={{0,2},{1,3},{2,0},{3,1},{4,6},{5,7},{6,4},{7,5},{8,10},{9,11},{10,... | collective-permute-start | bytes 6291464 | tf_op jit(solution)/shard_map/ppermute | solution.py:40
  87.9 39.0 %collective-permute-start.15 = (bf16[1024,512]{1,0:T(8,128)(2,1)}, bf16[1024,512]{1,0:T(8,128)(2,1)}, u32[]{:S(2)}, u32[]{:S(2)}) collective-permute-start(bf16[1024,512]{1,0:T(8,128)(2,1)} %collective-permute-done.5.b_ref.a_ref.refs_7_), channel_id=1, source_target_pairs={{8,0},{12,4},{16,8},{20,12},{24,16},{28,20},{9,1},{13,5},{17,9},{2... | collective-permute-start | bytes 3145736 | tf_op jit(solution)/shard_map/ppermute | solution.py:45
  264.3 40.0 %collective-permute-start.35 = (bf16[1376,512]{1,0:T(8,128)(2,1)}, bf16[1376,512]{1,0:T(8,128)(2,1)S(1)}, u32[]{:S(2)}, u32[]{:S(2)}) collective-permute-start(bf16[1376,512]{1,0:T(8,128)(2,1)} %get-tuple-element.364.a_ref), channel_id=1, source_target_pairs={{0,8},{4,12},{24,16},{28,20},{1,9},{5,13},{25,17},{29,21},{2,10},{... | collective-permute-start | bytes 4227080 | tf_op jit(solution)/shard_map/ppermute | solution.py:55
  320.1 374.0 %reduce-scatter.2.cloned.1.call-start = ((), (), s32[]{:S(2)}) async-start(), calls=%async_computation.2 | async-start | bytes 5242880 | tf_op jit(solution)/shard_map/reduce_scatter | solution.py:1194
  327.6 67.7 %collective-permute-start.45 = (bf16[1376,512]{1,0:T(8,128)(2,1)}, bf16[1376,512]{1,0:T(8,128)(2,1)}, u32[]{:S(2)}, u32[]{:S(2)}) collective-permute-start(bf16[1376,512]{1,0:T(8,128)(2,1)} %fold.21.a_ref), channel_id=1, source_target_pairs={{8,16},{12,20},{16,8},{20,12},{9,17},{13,21},{17,9},{21,13},{10,18... | collective-permute-start | bytes 4227080 | tf_op jit(solution)/shard_map/ppermute | solution.py:55
  329.3 71.1 %collective-permute-start.44 = (bf16[1376,512]{1,0:T(8,128)(2,1)}, bf16[1376,512]{1,0:T(8,128)(2,1)}, u32[]{:S(2)}, u32[]{:S(2)}) collective-permute-start(bf16[1376,512]{1,0:T(8,128)(2,1)} %get-tuple-element.393.a_ref), channel_id=1, source_target_pairs={{0,8},{4,12},{24,16},{28,20},{1,9},{5,13},{25,17},{29,21},{2,10},{... | collective-permute-start | bytes 4227080 | tf_op jit(solution)/shard_map/ppermute | solution.py:55
  348.5 67.7 %collective-permute-start.46 = (bf16[1376,512]{1,0:T(8,128)(2,1)}, bf16[1376,512]{1,0:T(8,128)(2,1)}, u32[]{:S(2)}, u32[]{:S(2)}) collective-permute-start(bf16[1376,512]{1,0:T(8,128)(2,1)} %fold.22.a_ref), channel_id=1, source_target_pairs={{8,0},{12,4},{16,24},{20,28},{9,1},{13,5},{17,25},{21,29},{10,2},{... | collective-permute-start | bytes 4227080 | tf_op jit(solution)/shard_map/ppermute | solution.py:55
  362.6 83.0 %collective-permute-start.43 = (bf16[1376,512]{1,0:T(8,128)(2,1)}, bf16[1376,512]{1,0:T(8,128)(2,1)}, u32[]{:S(2)}, u32[]{:S(2)}) collective-permute-start(bf16[1376,512]{1,0:T(8,128)(2,1)} %fold.23.a_ref), channel_id=1, source_target_pairs={{8,16},{12,20},{16,8},{20,12},{9,17},{13,21},{17,9},{21,13},{10,18... | collective-permute-start | bytes 4227080 | tf_op jit(solution)/shard_map/ppermute | solution.py:55
  364.5 86.8 %collective-permute-start.41 = (bf16[1088,512]{1,0:T(8,128)(2,1)S(1)}, bf16[1088,512]{1,0:T(8,128)(2,1)}, u32[]{:S(2)}, u32[]{:S(2)}) collective-permute-start(bf16[1088,512]{1,0:T(8,128)(2,1)S(1)} %join_true.1.g_ref.a_ref.refs_0_.refs_10_), channel_id=1, source_target_pairs={{8,0},{12,4},{16,8},{20,12},{24,16},{28,20},{9,1},{13,5},{17,9},{2... | collective-permute-start | bytes 3342344 | tf_op jit(solution)/shard_map/ppermute | solution.py:45
  378.1 471.0 %all-gather.8.cloned.1.call-start = ((), (), s32[]{:S(2)}) async-start(), calls=%async_computation.4 | async-start | bytes 5242880 | tf_op jit(solution)/shard_map/all_gather | solution.py:1282
  399.1 70.9 %collective-permute-start.52 = (bf16[1376,512]{1,0:T(8,128)(2,1)}, bf16[1376,512]{1,0:T(8,128)(2,1)}, u32[]{:S(2)}, u32[]{:S(2)}) collective-permute-start(bf16[1376,512]{1,0:T(8,128)(2,1)} %fold.24.a_ref), channel_id=1, source_target_pairs={{8,0},{12,4},{16,24},{20,28},{9,1},{13,5},{17,25},{21,29},{10,2},{... | collective-permute-start | bytes 4227080 | tf_op jit(solution)/shard_map/ppermute | solution.py:55
  421.8 51.7 %collective-permute-start.51 = (bf16[1024,512]{1,0:T(8,128)(2,1)}, bf16[1024,512]{1,0:T(8,128)(2,1)}, u32[]{:S(2)}, u32[]{:S(2)}) collective-permute-start(bf16[1024,512]{1,0:T(8,128)(2,1)} %fusion.20), channel_id=1, source_target_pairs={{0,4},{4,0},{8,12},{12,8},{16,20},{20,16},{24,28},{28,24},{1,5},{5... | collective-permute-start | bytes 3145736 | tf_op jit(solution)/shard_map/ppermute | solution.py:50
  422.1 56.6 %collective-permute-start.50 = (bf16[1376,512]{1,0:T(8,128)(2,1)}, bf16[1376,512]{1,0:T(8,128)(2,1)}, u32[]{:S(2)}, u32[]{:S(2)}) collective-permute-start(bf16[1376,512]{1,0:T(8,128)(2,1)} %get-tuple-element.409.a_ref), channel_id=1, source_target_pairs={{0,8},{4,12},{24,16},{28,20},{1,9},{5,13},{25,17},{29,21},{2,10},{... | collective-permute-start | bytes 4227080 | tf_op jit(solution)/shard_map/ppermute | solution.py:55
  451.3 42.6 %collective-permute-start.48 = (bf16[1088,512]{1,0:T(8,128)(2,1)}, bf16[1088,512]{1,0:T(8,128)(2,1)}, u32[]{:S(2)}, u32[]{:S(2)}) collective-permute-start(bf16[1088,512]{1,0:T(8,128)(2,1)} %collective-permute-done.41.b_ref.a_ref.refs_2_.refs_12_), channel_id=1, source_target_pairs={{8,0},{12,4},{16,8},{20,12},{24,16},{28,20},{9,1},{13,5},{17,9},{2... | collective-permute-start | bytes 3342344 | tf_op jit(solution)/shard_map/ppermute | solution.py:45
  478.7 41.0 %collective-permute-start.55 = (bf16[1376,512]{1,0:T(8,128)(2,1)}, bf16[1376,512]{1,0:T(8,128)(2,1)S(1)}, u32[]{:S(2)}, u32[]{:S(2)}) collective-permute-start(bf16[1376,512]{1,0:T(8,128)(2,1)} %fold.26.a_ref), channel_id=1, source_target_pairs={{8,0},{12,4},{16,24},{20,28},{9,1},{13,5},{17,25},{21,29},{10,2},{... | collective-permute-start | bytes 4227080 | tf_op jit(solution)/shard_map/ppermute | solution.py:55
  500.7 50.1 %collective-permute-start.47 = (bf16[1088,512]{1,0:T(8,128)(2,1)}, bf16[1088,512]{1,0:T(8,128)(2,1)}, u32[]{:S(2)}, u32[]{:S(2)}) collective-permute-start(bf16[1088,512]{1,0:T(8,128)(2,1)} %pick.23), channel_id=1, source_target_pairs={{0,4},{4,0},{8,12},{12,8},{16,20},{20,16},{24,28},{28,24},{1,5},{5... | collective-permute-start | bytes 3342344 | tf_op jit(solution)/shard_map/ppermute | solution.py:50
  504.0 47.1 %collective-permute-start.53 = (bf16[1088,512]{1,0:T(8,128)(2,1)}, bf16[1088,512]{1,0:T(8,128)(2,1)}, u32[]{:S(2)}, u32[]{:S(2)}) collective-permute-start(bf16[1088,512]{1,0:T(8,128)(2,1)} %pick.25), channel_id=1, source_target_pairs={{0,4},{4,0},{8,12},{12,8},{16,20},{20,16},{24,28},{28,24},{1,5},{5... | collective-permute-start | bytes 3342344 | tf_op jit(solution)/shard_map/ppermute | solution.py:50
  505.9 63.4 %collective-permute-start.58 = (bf16[1376,512]{1,0:T(8,128)(2,1)}, bf16[1376,512]{1,0:T(8,128)(2,1)}, u32[]{:S(2)}, u32[]{:S(2)}) collective-permute-start(bf16[1376,512]{1,0:T(8,128)(2,1)} %fold.27.a_ref), channel_id=1, source_target_pairs={{8,16},{12,20},{16,8},{20,12},{9,17},{13,21},{17,9},{21,13},{10,18... | collective-permute-start | bytes 4227080 | tf_op jit(solution)/shard_map/ppermute | solution.py:55
  520.8 52.4 %collective-permute-start.57 = (bf16[1024,512]{1,0:T(8,128)(2,1)}, bf16[1024,512]{1,0:T(8,128)(2,1)}, u32[]{:S(2)}, u32[]{:S(2)}) collective-permute-start(bf16[1024,512]{1,0:T(8,128)(2,1)} %add_convert_fusion.5.a_ref), channel_id=1, source_target_pairs={{0,8},{4,12},{24,16},{28,20},{1,9},{5,13},{25,17},{29,21},{2,10},{... | collective-permute-start | bytes 3145736 | tf_op jit(solution)/shard_map/ppermute | solution.py:55
  550.8 46.8 %collective-permute-start.75 = (bf16[1376,512]{1,0:T(8,128)(2,1)S(1)}, bf16[1376,512]{1,0:T(8,128)(2,1)S(1)}, u32[]{:S(2)}, u32[]{:S(2)}) collective-permute-start(bf16[1376,512]{1,0:T(8,128)(2,1)S(1)} %copy-done.46), channel_id=1, source_target_pairs={{0,4},{4,0},{8,12},{12,8},{16,20},{20,16},{24,28},{28,24},{1,5},{5... | collective-permute-start | bytes 4227080 | tf_op jit(solution)/shard_map/ppermute | solution.py:50
  551.1 47.9 %collective-permute-start.61 = (bf16[1376,512]{1,0:T(8,128)(2,1)}, bf16[1376,512]{1,0:T(8,128)(2,1)S(1)}, u32[]{:S(2)}, u32[]{:S(2)}) collective-permute-start(bf16[1376,512]{1,0:T(8,128)(2,1)} %fold.28.a_ref), channel_id=1, source_target_pairs={{8,0},{12,4},{16,24},{20,28},{9,1},{13,5},{17,25},{21,29},{10,2},{... | collective-permute-start | bytes 4227080 | tf_op jit(solution)/shard_map/ppermute | solution.py:55
  556.3 51.9 %collective-permute-start.76 = (bf16[1376,512]{1,0:T(8,128)(2,1)}, bf16[1376,512]{1,0:T(8,128)(2,1)}, u32[]{:S(2)}, u32[]{:S(2)}) collective-permute-start(bf16[1376,512]{1,0:T(8,128)(2,1)} %pick.24.refs_1_), channel_id=1, source_target_pairs={{0,4},{4,0},{8,12},{12,8},{16,20},{20,16},{24,28},{28,24},{1,5},{5... | collective-permute-start | bytes 4227080 | tf_op jit(solution)/shard_map/ppermute | solution.py:50
  600.1 60.3 %collective-permute-start.74 = (bf16[1376,512]{1,0:T(8,128)(2,1)}, bf16[1376,512]{1,0:T(8,128)(2,1)}, u32[]{:S(2)}, u32[]{:S(2)}) collective-permute-start(bf16[1376,512]{1,0:T(8,128)(2,1)} %fold.30.a_ref), channel_id=1, source_target_pairs={{8,0},{12,4},{16,24},{20,28},{9,1},{13,5},{17,25},{21,29},{10,2},{... | collective-permute-start | bytes 4227080 | tf_op jit(solution)/shard_map/ppermute | solution.py:55
  608.2 50.9 %collective-permute-start.73 = (bf16[1024,512]{1,0:T(8,128)(2,1)}, bf16[1024,512]{1,0:T(8,128)(2,1)}, u32[]{:S(2)}, u32[]{:S(2)}) collective-permute-start(bf16[1024,512]{1,0:T(8,128)(2,1)} %fold.31.a_ref), channel_id=1, source_target_pairs={{8,16},{12,20},{16,8},{20,12},{9,17},{13,21},{17,9},{21,13},{10,18... | collective-permute-start | bytes 3145736 | tf_op jit(solution)/shard_map/ppermute | solution.py:55
  630.1 49.3 %collective-permute-start.70 = (bf16[1376,512]{1,0:T(8,128)(2,1)S(1)}, bf16[1376,512]{1,0:T(8,128)(2,1)}, u32[]{:S(2)}, u32[]{:S(2)}) collective-permute-start(bf16[1376,512]{1,0:T(8,128)(2,1)S(1)} %copy-done.49), channel_id=1, source_target_pairs={{0,4},{4,0},{8,12},{12,8},{16,20},{20,16},{24,28},{28,24},{1,5},{5... | collective-permute-start | bytes 4227080 | tf_op jit(solution)/shard_map/ppermute | solution.py:50
  694.0 160.8 %all-gather.6.cloned.1.call-start = ((), (), s32[]{:S(2)}) async-start(), calls=%async_computation.3 | async-start | bytes 5242880 | tf_op jit(solution)/shard_map/all_gather | solution.py:1282
  704.0 50.1 %collective-permute-start.77 = (bf16[1024,512]{1,0:T(8,128)(2,1)}, bf16[1024,512]{1,0:T(8,128)(2,1)S(1)}, u32[]{:S(2)}, u32[]{:S(2)}) collective-permute-start(bf16[1024,512]{1,0:T(8,128)(2,1)} %fold.34.a_ref), channel_id=1, source_target_pairs={{8,0},{12,4},{16,24},{20,28},{9,1},{13,5},{17,25},{21,29},{10,2},{... | collective-permute-start | bytes 3145736 | tf_op jit(solution)/shard_map/ppermute | solution.py:55
  705.3 51.7 %collective-permute-start.84 = (bf16[1376,512]{1,0:T(8,128)(2,1)}, bf16[1376,512]{1,0:T(8,128)(2,1)S(1)}, u32[]{:S(2)}, u32[]{:S(2)}) collective-permute-start(bf16[1376,512]{1,0:T(8,128)(2,1)} %copy-done.50), channel_id=1, source_target_pairs={{0,4},{4,0},{8,12},{12,8},{16,20},{20,16},{24,28},{28,24},{1,5},{5... | collective-permute-start | bytes 4227080 | tf_op jit(solution)/shard_map/ppermute | solution.py:50
  757.0 47.5 %collective-permute-start.87 = (bf16[1024,512]{1,0:T(8,128)(2,1)S(1)}, bf16[1024,512]{1,0:T(8,128)(2,1)S(1)}, u32[]{:S(2)}, u32[]{:S(2)}) collective-permute-start(bf16[1024,512]{1,0:T(8,128)(2,1)S(1)} %fold.38.a_ref), channel_id=1, source_target_pairs={{8,0},{12,4},{16,24},{20,28},{9,1},{13,5},{17,25},{21,29},{10,2},{... | collective-permute-start | bytes 3145736 | tf_op jit(solution)/shard_map/ppermute | solution.py:55
  783.5 41.2 %collective-permute-start.89 = (bf16[1024,512]{1,0:T(8,128)(2,1)S(1)}, bf16[1024,512]{1,0:T(8,128)(2,1)S(1)}, u32[]{:S(2)}, u32[]{:S(2)}) collective-permute-start(bf16[1024,512]{1,0:T(8,128)(2,1)S(1)} %fold.39.a_ref), channel_id=1, source_target_pairs={{8,0},{12,4},{16,24},{20,28},{9,1},{13,5},{17,25},{21,29},{10,2},{... | collective-permute-start | bytes 3145736 | tf_op jit(solution)/shard_map/ppermute | solution.py:55
  (171 other events, 2120.8 us)
Sparse Core Ops, SparseCore 0:
  320.2 57.7 all-gather.3
  381.6 68.4 reduce-scatter.1
  694.2 50.9 all-gather.7
  747.6 53.0 all-gather.5
